TPU v7x, 256 devices: a whole 4x4x8 slice. The times are simulated.
256 devices in a mesh: row: 8 (over z), col: 32 (over x, y, core).
Axes of the slice: x: 4, y: 4, z: 8, core: 2. Of those that a mesh axis runs over, the one named last changes fastest.
Arguments:
- xn: bfloat16 [1024, 2048], P('col', 'row'), may hold values from -6 to 6
- w_qkv: bfloat16 [2048, 6144], P('row', 'col'), may hold values from -0.125 to 0.125
- w_out: bfloat16 [2048, 2048], P('col', 'row'), may hold values from -0.125 to 0.125
- pool: bfloat16 [2048, 64, 4096], P('row', None, 'col'), may hold values from -136 to 136
- page_table: int32 [1024, 64], P('row'), may hold values from 0 to 271
- lengths: int32 [1024], P('row'), may hold values from 1 to 4096, 98304 in all
- mig_src: int32 [128], replicated, may hold values from 0 to 2047, as said below
- deal: int32 [1024], replicated, may hold values from 0 to 1023, each once
Outputs:
- attended: bfloat16 [1024, 2048], P('col', 'row')
- landed: bfloat16 [128, 64, 4096], P('row', None, 'col')
Inputs may be any that keep to these rules, and one draw needn't show every extreme that they name: `page_table`: page ids of a request refer to its own row block: below 256 its pool pages, from 256 its landing slots. `lengths`: the longest request has exactly 4096 cache tokens. `mig_src`: slot d belongs to row block d // 16; its source page lies in the pool pages of another row block. `deal`: a permutation of the requests.
All inputs are finite; a program needn't handle non-finite values. No bound on the sum of `lengths` on one device may be relied on, other than what follows from the above.
Results may differ from a plain program's by a relative error of at most 0.02.
Values may be sent and summed in bfloat16 or wider, within the bound.
A program may use at most 128 MiB of HBM per device.

v0:
```python
import jax
import jax.numpy as jnp
from jax import lax
from jax.sharding import PartitionSpec as P

HEAD_DIM = 64
PAGE = 64


theta_base = 130000.0
neg_large = -1e30


def rotate(values, positions):
    half = values.shape[-1] // 2
    freqs = theta_base ** (-(jnp.arange(half, dtype=jnp.float32) * 2.0 / values.shape[-1]))
    angles = positions.astype(jnp.float32)[:, None, None] * freqs[None, None, :]
    cosine = jnp.cos(angles)
    sine = jnp.sin(angles)
    first = values[..., :half]
    second = values[..., half:]
    return jnp.concatenate(
        [first * cosine - second * sine, second * cosine + first * sine], axis=-1
    )


def attend(query, key_new, value_new, table, lens, key_pool, value_pool):
    req_count = query.shape[0]
    heads_here = query.shape[1]
    pages_all = table.shape[1]
    pages_block = min(pages_all, max(1, 512 // PAGE))
    block_len = pages_block * PAGE
    longest = jnp.max(lens)
    block_count = (longest + block_len - 1) // block_len
    positions = jnp.arange(block_len, dtype=jnp.int32)

    def score_block(block_no, scores):
        page_ids = lax.dynamic_slice_in_dim(table, block_no * pages_block, pages_block, 1)
        keys = key_pool[page_ids].reshape(req_count, block_len, heads_here, HEAD_DIM)
        block_scores = (
            jnp.einsum("rhe,rthe->rht", query, keys, preferred_element_type=jnp.float32) * 0.125
        )
        valid = (block_no * block_len + positions)[None, None, :] < lens[:, None, None]
        block_scores = jnp.where(valid, block_scores, neg_large)
        return lax.dynamic_update_slice_in_dim(scores, block_scores, block_no * block_len, 2)

    initial = jnp.full((req_count, heads_here, pages_all * PAGE), neg_large, jnp.float32)
    scores = lax.fori_loop(0, block_count, score_block, initial)
    score_new = jnp.sum(query.astype(jnp.float32) * key_new.astype(jnp.float32), axis=-1) * 0.125
    top = jnp.maximum(jnp.max(scores, axis=2), score_new)
    expo_new = jnp.exp(score_new - top)
    total = jnp.sum(jnp.exp(scores - top[..., None]), axis=2) + expo_new

    def value_block(block_no, numer):
        block_scores = lax.dynamic_slice_in_dim(scores, block_no * block_len, block_len, 2)
        weights = jnp.exp(block_scores - top[..., None]).astype(jnp.bfloat16)
        page_ids = lax.dynamic_slice_in_dim(table, block_no * pages_block, pages_block, 1)
        values = value_pool[page_ids].reshape(req_count, block_len, heads_here, HEAD_DIM)
        return numer + jnp.einsum(
            "rht,rthe->rhe", weights, values, preferred_element_type=jnp.float32
        )

    numer = lax.fori_loop(
        0, block_count, value_block, jnp.zeros((req_count, heads_here, HEAD_DIM), jnp.float32)
    )
    weight_new = lax.optimization_barrier(expo_new.astype(jnp.bfloat16)).astype(jnp.float32)
    numer = numer + weight_new[..., None] * value_new.astype(jnp.float32)
    return (numer / total[..., None]).astype(jnp.bfloat16)


def on_device(xn, w_qkv, w_out, pool, page_table, lengths, mig_src, deal):
    heads_here = w_out.shape[0] // HEAD_DIM
    rows_all = xn.shape[0] * lax.axis_size("col")
    row_count = lax.axis_size("row")
    req_row = rows_all // row_count
    inverse = jnp.zeros((rows_all,), jnp.int32).at[deal].set(jnp.arange(rows_all, dtype=jnp.int32))
    gathered = lax.all_gather(xn, "col", axis=0, tiled=True)
    chosen = inverse
    projected = lax.psum_scatter(
        jnp.dot(jnp.take(gathered, chosen, axis=0), w_qkv, preferred_element_type=jnp.float32),
        "row",
        scatter_dimension=0,
        tiled=True,
    )
    projected = projected.reshape(req_row, heads_here, 3, HEAD_DIM)
    query = rotate(projected[:, :, 0], lengths).astype(jnp.bfloat16)
    key_new = rotate(projected[:, :, 1], lengths).astype(jnp.bfloat16)
    value_new = projected[:, :, 2].astype(jnp.bfloat16)
    my_row = lax.axis_index("row")
    pool_dev = pool.shape[0]
    land_dev = mig_src.shape[0] // row_count
    source_row = mig_src // pool_dev
    local_page = jnp.clip(mig_src - my_row * pool_dev, 0, pool_dev - 1)
    outgoing = jnp.where(
        (source_row == my_row)[:, None, None],
        jnp.take(pool, local_page, axis=0),
        jnp.zeros((), jnp.bfloat16),
    )
    outgoing = outgoing.reshape(row_count, land_dev, pool.shape[1], pool.shape[2])
    received = lax.all_to_all(outgoing, "row", split_axis=0, concat_axis=0, tiled=True)
    my_sources = lax.dynamic_slice_in_dim(source_row, my_row * land_dev, land_dev)
    landed = received[my_sources, jnp.arange(land_dev)]
    combined = jnp.concatenate([pool, landed], axis=0)
    combined = combined.reshape(combined.shape[0], PAGE, heads_here, 2, HEAD_DIM)
    key_pool = combined[:, :, :, 0]
    value_pool = combined[:, :, :, 1]
    mixed = attend(query, key_new, value_new, page_table, lengths, key_pool, value_pool)
    mixed = mixed.reshape(req_row, heads_here * HEAD_DIM)
    mixed_all = lax.all_gather(mixed, "row", axis=0, tiled=True)
    chosen = deal
    attended = lax.psum_scatter(
        jnp.dot(
            jnp.take(mixed_all, chosen, axis=0), w_out, preferred_element_type=jnp.float32
        ).astype(jnp.bfloat16),
        "col",
        scatter_dimension=0,
        tiled=True,
    )
    return (attended, landed)


def solution(mesh):
    placed = (
        P("col", "row"),
        P("row", "col"),
        P("col", "row"),
        P("row", None, "col"),
        P("row", None),
        P("row"),
        P(),
        P(),
    )
    return jax.shard_map(
        on_device,
        mesh=mesh,
        in_specs=placed,
        out_specs=(P("col", "row"), P("row", None, "col")),
        check_vma=False,
    )
```

profile of v0, /device:TPU:1, one launch (start us, length us, event | category | flops | bytes accessed | tf_op | source)
XLA Modules:
  0.0 794.2 jit_solution(766521219525709486)
XLA Ops:
  8.1 3.1 gather_fusion.2
  12.8 9.0 %all-to-all-start = ((bf16[8,16,64,128]{3,2,1,0:T(8,128)(2,1)}), bf16[8,16,64,128]{3,2,1,0:T(8,128)(2,1)S(1)}, u32[]{:S(2)}, u32[]{:S(2)}) async-start(bf16[8,16,64,128]{3,2,1,0:T(8,128)(2,1)} %select_select_fusion), calls=%async_computation | async-start | bytes 4194304 | tf_op jit(solution)/shard_map/all_to_all | solution.py:100
  22.5 4.3 scatter_custom_fusion
  26.8 25.9 %all_gather.6 = bf16[1024,256]{1,0:T(8,128)(2,1)S(1)} all-gather(bf16[32,256]{1,0:T(8,128)(2,1)S(1)} %copy-done.6), channel_id=1, replica_groups=mesh['row'=8,'col'=32] {'col'}, dimensions={0}, use_global_device_ids=true | all-gather | bytes 540672 | tf_op jit(solution)/shard_map/all_gather | solution.py:77
  52.7 3.9 gather_fusion.4
  59.4 6.9 copy.39
  67.1 23.5 %reduce-scatter.3.cloned.1.call-done = f32[128,192]{0,1:T(8,128)} async-done(((f32[1024,192]{0,1:T(8,128)}), f32[128,192]{0,1:T(8,128)}) %reduce-scatter.3.cloned.1.call-update) | async-done | bytes 98320 | tf_op jit(solution)/shard_map/reduce_scatter | solution.py:79
  93.2 3.3 pad_maximum_fusion
  96.6 2.4 slice_bitcast_fusion
  99.0 3.5 broadcast_in_dim.86
  102.5 261.0 %while.22 = (s32[]{:T(128)}, f32[128,1,4096]{2,1,0:T(1,128)}, s32[]{:T(128)}, s32[128]{0:T(128)S(1)}, s32[128,64]{1,0:T(8,128)S(1)}, /*index=5*/bf16[272,64,1,64...) while((s32[]{:T(128)}, f32[128,1,4096]{2,1,0:T(1,128)}, ...), condition=%wide.region_4.5_spmd.clone, body=%wide.region_3.4_spmd.clone.sunk | while | flops 8589834 | bytes 31015652 | solution.py:48
  102.7 9.9 %copy.78 = bf16[272,64,64]{2,1,0:T(8,128)(2,1)} copy(bf16[272,64,64]{0,2,1:T(8,128)(2,1)} %bitcast.89) | data formatting | bytes 4456448 | tf_op jit(solution)/shard_map
  112.6 15.7 %gather_fusion.1 = bf16[1024,64,64]{2,1,0:T(8,128)(2,1)} fusion(bf16[272,64,64]{2,1,0:T(8,128)(2,1)} %copy.78, s32[1024]{0:T(1024)S(1)} %broadcast_clamp_fusion.6), kind=kCustom, calls=%fused_computation.clone.clone.1 | custom fusion | bytes 16781312 | tf_op jit(solution)/shard_map/while/body/gather | solution.py:39
  129.1 8.1 %fusion.66 = f32[128,1,512]{2,1,0:T(1,128)S(1)} fusion(bf16[128,512,64]{2,1,0:T(8,128)(2,1)} %bitcast.87, bf16[128,64,1]{1,2,0:T(2,128)(2,1)} %copy.79), kind=kOutput, calls=%fused_computation.98.clone.1 | convolution fusion | flops 8388608 | bytes 8667136 | tf_op jit(solution)/shard_map/while/body/rhe,rthe->rht/dot_general | solution.py:41
  138.0 1.9 reshape_dynamic-update-slice_fusion.2
  140.0 9.9 %copy.78 = bf16[272,64,64]{2,1,0:T(8,128)(2,1)} copy(bf16[272,64,64]{0,2,1:T(8,128)(2,1)} %bitcast.89) | data formatting | bytes 4456448 | tf_op jit(solution)/shard_map
  149.9 15.7 %gather_fusion.1 = bf16[1024,64,64]{2,1,0:T(8,128)(2,1)} fusion(bf16[272,64,64]{2,1,0:T(8,128)(2,1)} %copy.78, s32[1024]{0:T(1024)S(1)} %broadcast_clamp_fusion.6), kind=kCustom, calls=%fused_computation.clone.clone.1 | custom fusion | bytes 16781312 | tf_op jit(solution)/shard_map/while/body/gather | solution.py:39
  166.4 8.1 %fusion.66 = f32[128,1,512]{2,1,0:T(1,128)S(1)} fusion(bf16[128,512,64]{2,1,0:T(8,128)(2,1)} %bitcast.87, bf16[128,64,1]{1,2,0:T(2,128)(2,1)} %copy.79), kind=kOutput, calls=%fused_computation.98.clone.1 | convolution fusion | flops 8388608 | bytes 8667136 | tf_op jit(solution)/shard_map/while/body/rhe,rthe->rht/dot_general | solution.py:41
  175.2 1.9 reshape_dynamic-update-slice_fusion.2
  177.3 9.9 %copy.78 = bf16[272,64,64]{2,1,0:T(8,128)(2,1)} copy(bf16[272,64,64]{0,2,1:T(8,128)(2,1)} %bitcast.89) | data formatting | bytes 4456448 | tf_op jit(solution)/shard_map
  187.2 15.7 %gather_fusion.1 = bf16[1024,64,64]{2,1,0:T(8,128)(2,1)} fusion(bf16[272,64,64]{2,1,0:T(8,128)(2,1)} %copy.78, s32[1024]{0:T(1024)S(1)} %broadcast_clamp_fusion.6), kind=kCustom, calls=%fused_computation.clone.clone.1 | custom fusion | bytes 16781312 | tf_op jit(solution)/shard_map/while/body/gather | solution.py:39
  203.7 8.1 %fusion.66 = f32[128,1,512]{2,1,0:T(1,128)S(1)} fusion(bf16[128,512,64]{2,1,0:T(8,128)(2,1)} %bitcast.87, bf16[128,64,1]{1,2,0:T(2,128)(2,1)} %copy.79), kind=kOutput, calls=%fused_computation.98.clone.1 | convolution fusion | flops 8388608 | bytes 8667136 | tf_op jit(solution)/shard_map/while/body/rhe,rthe->rht/dot_general | solution.py:41
  212.5 1.9 reshape_dynamic-update-slice_fusion.2
  214.6 9.9 %copy.78 = bf16[272,64,64]{2,1,0:T(8,128)(2,1)} copy(bf16[272,64,64]{0,2,1:T(8,128)(2,1)} %bitcast.89) | data formatting | bytes 4456448 | tf_op jit(solution)/shard_map
  224.5 15.7 %gather_fusion.1 = bf16[1024,64,64]{2,1,0:T(8,128)(2,1)} fusion(bf16[272,64,64]{2,1,0:T(8,128)(2,1)} %copy.78, s32[1024]{0:T(1024)S(1)} %broadcast_clamp_fusion.6), kind=kCustom, calls=%fused_computation.clone.clone.1 | custom fusion | bytes 16781312 | tf_op jit(solution)/shard_map/while/body/gather | solution.py:39
  241.0 8.1 %fusion.66 = f32[128,1,512]{2,1,0:T(1,128)S(1)} fusion(bf16[128,512,64]{2,1,0:T(8,128)(2,1)} %bitcast.87, bf16[128,64,1]{1,2,0:T(2,128)(2,1)} %copy.79), kind=kOutput, calls=%fused_computation.98.clone.1 | convolution fusion | flops 8388608 | bytes 8667136 | tf_op jit(solution)/shard_map/while/body/rhe,rthe->rht/dot_general | solution.py:41
  249.9 1.9 reshape_dynamic-update-slice_fusion.2
  251.9 9.9 %copy.78 = bf16[272,64,64]{2,1,0:T(8,128)(2,1)} copy(bf16[272,64,64]{0,2,1:T(8,128)(2,1)} %bitcast.89) | data formatting | bytes 4456448 | tf_op jit(solution)/shard_map
  261.8 15.7 %gather_fusion.1 = bf16[1024,64,64]{2,1,0:T(8,128)(2,1)} fusion(bf16[272,64,64]{2,1,0:T(8,128)(2,1)} %copy.78, s32[1024]{0:T(1024)S(1)} %broadcast_clamp_fusion.6), kind=kCustom, calls=%fused_computation.clone.clone.1 | custom fusion | bytes 16781312 | tf_op jit(solution)/shard_map/while/body/gather | solution.py:39
  278.3 8.1 %fusion.66 = f32[128,1,512]{2,1,0:T(1,128)S(1)} fusion(bf16[128,512,64]{2,1,0:T(8,128)(2,1)} %bitcast.87, bf16[128,64,1]{1,2,0:T(2,128)(2,1)} %copy.79), kind=kOutput, calls=%fused_computation.98.clone.1 | convolution fusion | flops 8388608 | bytes 8667136 | tf_op jit(solution)/shard_map/while/body/rhe,rthe->rht/dot_general | solution.py:41
  289.2 9.9 %copy.78 = bf16[272,64,64]{2,1,0:T(8,128)(2,1)} copy(bf16[272,64,64]{0,2,1:T(8,128)(2,1)} %bitcast.89) | data formatting | bytes 4456448 | tf_op jit(solution)/shard_map
  299.0 15.7 %gather_fusion.1 = bf16[1024,64,64]{2,1,0:T(8,128)(2,1)} fusion(bf16[272,64,64]{2,1,0:T(8,128)(2,1)} %copy.78, s32[1024]{0:T(1024)S(1)} %broadcast_clamp_fusion.6), kind=kCustom, calls=%fused_computation.clone.clone.1 | custom fusion | bytes 16781312 | tf_op jit(solution)/shard_map/while/body/gather | solution.py:39
  315.5 8.1 %fusion.66 = f32[128,1,512]{2,1,0:T(1,128)S(1)} fusion(bf16[128,512,64]{2,1,0:T(8,128)(2,1)} %bitcast.87, bf16[128,64,1]{1,2,0:T(2,128)(2,1)} %copy.79), kind=kOutput, calls=%fused_computation.98.clone.1 | convolution fusion | flops 8388608 | bytes 8667136 | tf_op jit(solution)/shard_map/while/body/rhe,rthe->rht/dot_general | solution.py:41
  324.4 1.9 reshape_dynamic-update-slice_fusion.2
  326.5 9.9 %copy.78 = bf16[272,64,64]{2,1,0:T(8,128)(2,1)} copy(bf16[272,64,64]{0,2,1:T(8,128)(2,1)} %bitcast.89) | data formatting | bytes 4456448 | tf_op jit(solution)/shard_map
  336.3 15.7 %gather_fusion.1 = bf16[1024,64,64]{2,1,0:T(8,128)(2,1)} fusion(bf16[272,64,64]{2,1,0:T(8,128)(2,1)} %copy.78, s32[1024]{0:T(1024)S(1)} %broadcast_clamp_fusion.6), kind=kCustom, calls=%fused_computation.clone.clone.1 | custom fusion | bytes 16781312 | tf_op jit(solution)/shard_map/while/body/gather | solution.py:39
  352.8 8.1 %fusion.66 = f32[128,1,512]{2,1,0:T(1,128)S(1)} fusion(bf16[128,512,64]{2,1,0:T(8,128)(2,1)} %bitcast.87, bf16[128,64,1]{1,2,0:T(2,128)(2,1)} %copy.79), kind=kOutput, calls=%fused_computation.98.clone.1 | convolution fusion | flops 8388608 | bytes 8667136 | tf_op jit(solution)/shard_map/while/body/rhe,rthe->rht/dot_general | solution.py:41
  363.6 3.1 reduce_max.21
  366.7 4.6 exponential_reduce_fusion
  371.4 232.9 %while.21 = (s32[]{:T(128)}, f32[128,1,64]{2,1,0:T(1,128)S(1)}, s32[]{:T(128)}, f32[128,1,4096]{2,1,0:T(1,128)}, f32[128,1]{0,1:T(1,128)S(1)}, /*index=5*/s32[12...) while((s32[]{:T(128)}, f32[128,1,64]{2,1,0:T(1,128)S(1)}, ...), condition=%wide.region_8.9_spmd, body=%wide.region_7.8_spmd.sunk | while | flops 8531978 | bytes 30765792 | solution.py:63
  371.6 9.2 %copy.76 = bf16[272,64,64]{2,1,0:T(8,128)(2,1)} copy(bf16[272,64,64]{0,2,1:T(8,128)(2,1)S(1)} %bitcast.88) | data formatting | bytes 4456448 | tf_op jit(solution)/shard_map
  380.8 15.7 %gather_fusion = bf16[1024,64,64]{2,1,0:T(8,128)(2,1)} fusion(bf16[272,64,64]{2,1,0:T(8,128)(2,1)} %copy.76, s32[1024]{0:T(1024)S(1)} %broadcast_clamp_fusion.5), kind=kCustom, calls=%fused_computation.1.clone.1 | custom fusion | bytes 16781312 | tf_op jit(solution)/shard_map/while/body/gather | solution.py:58
  397.6 7.1 convolution_add_fusion.2
  404.9 9.2 %copy.76 = bf16[272,64,64]{2,1,0:T(8,128)(2,1)} copy(bf16[272,64,64]{0,2,1:T(8,128)(2,1)S(1)} %bitcast.88) | data formatting | bytes 4456448 | tf_op jit(solution)/shard_map
  414.0 15.7 %gather_fusion = bf16[1024,64,64]{2,1,0:T(8,128)(2,1)} fusion(bf16[272,64,64]{2,1,0:T(8,128)(2,1)} %copy.76, s32[1024]{0:T(1024)S(1)} %broadcast_clamp_fusion.5), kind=kCustom, calls=%fused_computation.1.clone.1 | custom fusion | bytes 16781312 | tf_op jit(solution)/shard_map/while/body/gather | solution.py:58
  430.8 7.1 convolution_add_fusion.2
  438.1 9.2 %copy.76 = bf16[272,64,64]{2,1,0:T(8,128)(2,1)} copy(bf16[272,64,64]{0,2,1:T(8,128)(2,1)S(1)} %bitcast.88) | data formatting | bytes 4456448 | tf_op jit(solution)/shard_map
  447.3 15.7 %gather_fusion = bf16[1024,64,64]{2,1,0:T(8,128)(2,1)} fusion(bf16[272,64,64]{2,1,0:T(8,128)(2,1)} %copy.76, s32[1024]{0:T(1024)S(1)} %broadcast_clamp_fusion.5), kind=kCustom, calls=%fused_computation.1.clone.1 | custom fusion | bytes 16781312 | tf_op jit(solution)/shard_map/while/body/gather | solution.py:58
  464.1 7.1 convolution_add_fusion.2
  471.4 9.2 %copy.76 = bf16[272,64,64]{2,1,0:T(8,128)(2,1)} copy(bf16[272,64,64]{0,2,1:T(8,128)(2,1)S(1)} %bitcast.88) | data formatting | bytes 4456448 | tf_op jit(solution)/shard_map
  480.6 15.7 %gather_fusion = bf16[1024,64,64]{2,1,0:T(8,128)(2,1)} fusion(bf16[272,64,64]{2,1,0:T(8,128)(2,1)} %copy.76, s32[1024]{0:T(1024)S(1)} %broadcast_clamp_fusion.5), kind=kCustom, calls=%fused_computation.1.clone.1 | custom fusion | bytes 16781312 | tf_op jit(solution)/shard_map/while/body/gather | solution.py:58
  497.4 7.1 convolution_add_fusion.2
  504.7 9.2 %copy.76 = bf16[272,64,64]{2,1,0:T(8,128)(2,1)} copy(bf16[272,64,64]{0,2,1:T(8,128)(2,1)S(1)} %bitcast.88) | data formatting | bytes 4456448 | tf_op jit(solution)/shard_map
  513.8 15.7 %gather_fusion = bf16[1024,64,64]{2,1,0:T(8,128)(2,1)} fusion(bf16[272,64,64]{2,1,0:T(8,128)(2,1)} %copy.76, s32[1024]{0:T(1024)S(1)} %broadcast_clamp_fusion.5), kind=kCustom, calls=%fused_computation.1.clone.1 | custom fusion | bytes 16781312 | tf_op jit(solution)/shard_map/while/body/gather | solution.py:58
  530.6 7.1 convolution_add_fusion.2
  537.9 9.2 %copy.76 = bf16[272,64,64]{2,1,0:T(8,128)(2,1)} copy(bf16[272,64,64]{0,2,1:T(8,128)(2,1)S(1)} %bitcast.88) | data formatting | bytes 4456448 | tf_op jit(solution)/shard_map
  547.1 15.7 %gather_fusion = bf16[1024,64,64]{2,1,0:T(8,128)(2,1)} fusion(bf16[272,64,64]{2,1,0:T(8,128)(2,1)} %copy.76, s32[1024]{0:T(1024)S(1)} %broadcast_clamp_fusion.5), kind=kCustom, calls=%fused_computation.1.clone.1 | custom fusion | bytes 16781312 | tf_op jit(solution)/shard_map/while/body/gather | solution.py:58
  563.9 7.1 convolution_add_fusion.2
  571.2 9.2 %copy.76 = bf16[272,64,64]{2,1,0:T(8,128)(2,1)} copy(bf16[272,64,64]{0,2,1:T(8,128)(2,1)S(1)} %bitcast.88) | data formatting | bytes 4456448 | tf_op jit(solution)/shard_map
  580.4 15.7 %gather_fusion = bf16[1024,64,64]{2,1,0:T(8,128)(2,1)} fusion(bf16[272,64,64]{2,1,0:T(8,128)(2,1)} %copy.76, s32[1024]{0:T(1024)S(1)} %broadcast_clamp_fusion.5), kind=kCustom, calls=%fused_computation.1.clone.1 | custom fusion | bytes 16781312 | tf_op jit(solution)/shard_map/while/body/gather | solution.py:58
  597.2 7.1 convolution_add_fusion.2
  605.1 85.5 %all-gather = bf16[1024,1,64]{0,2,1:T(8,128)(2,1)S(1)} all-gather(bf16[128,1,64]{0,2,1:T(8,128)(2,1)S(1)} %fusion.16), channel_id=2, replica_groups=mesh['row'=8,'col'=32] {'row'}, dimensions={0}, use_global_device_ids=true | all-gather | bytes 147456 | tf_op jit(solution)/shard_map/all_gather | solution.py:109
  690.9 3.2 gather_fusion.5
  695.3 92.1 %reduce-scatter.5.cloned.1.call-done = bf16[32,256]{1,0:T(8,128)(2,1)} async-done(((bf16[1024,256]{1,0:T(8,128)(2,1)}), bf16[32,256]{1,0:T(8,128)(2,1)}) %reduce-scatter.5.cloned.1.call-update) | async-done | bytes 16400 | tf_op jit(solution)/shard_map/reduce_scatter | solution.py:111
  (134 shorter events, 35.4 us)
Async XLA Ops:
  7.2 49.5 %copy-start = (bf16[256,192]{0,1:T(8,128)(2,1)S(1)}, bf16[256,192]{0,1:T(8,128)(2,1)}, u32[]{:S(2)}) copy-start(bf16[256,192]{0,1:T(8,128)(2,1)} %param.13) | copy-start | bytes 294916
  11.2 10.7 %copy-start.7 = (s32[1024]{0:T(1024)S(1)}, s32[1024]{0:T(1024)}, u32[]{:S(2)}) copy-start(s32[1024]{0:T(1024)} %param.19) | copy-start | bytes 12292
  11.2 15.6 %copy-start.6 = (bf16[32,256]{1,0:T(8,128)(2,1)S(1)}, bf16[32,256]{1,0:T(8,128)(2,1)}, u32[]{:S(2)}) copy-start(bf16[32,256]{1,0:T(8,128)(2,1)} %param.12) | copy-start | bytes 49156
  12.8 78.7 %all-to-all-start = ((bf16[8,16,64,128]{3,2,1,0:T(8,128)(2,1)}), bf16[8,16,64,128]{3,2,1,0:T(8,128)(2,1)S(1)}, u32[]{:S(2)}, u32[]{:S(2)}) async-start(bf16[8,16,64,128]{3,2,1,0:T(8,128)(2,1)} %select_select_fusion), calls=%async_computation | async-start | bytes 4194304 | tf_op jit(solution)/shard_map/all_to_all | solution.py:100
  21.8 36.2 %copy-start.8 = (s32[128]{0:T(128)S(1)}, s32[128]{0:T(128)}, u32[]{:S(2)}) copy-start(s32[128]{0:T(128)} %param.17) | copy-start | bytes 1540
  21.8 68.7 %reduce-scatter.3.cloned.1.call-start = ((), (), s32[]{:S(2)}) async-start(), calls=%async_computation.3 | async-start | bytes 884736 | tf_op jit(solution)/shard_map/reduce_scatter | solution.py:79
  58.0 729.4 %reduce-scatter.5.cloned.1.call-start = ((), (), s32[]{:S(2)}) async-start(), calls=%async_computation.4 | async-start | bytes 540672 | tf_op jit(solution)/shard_map/reduce_scatter | solution.py:111
  59.4 6.9 copy-start.3
  92.2 4.4 copy-start.2
  371.3 319.5 %copy-start.5 = (s32[1024]{0:T(1024)S(1)}, s32[1024]{0:T(1024)}, u32[]{:S(2)}) copy-start(s32[1024]{0:T(1024)} %get-tuple-element.191) | copy-start | bytes 12292
  371.4 322.7 %copy-start.4 = (bf16[64,256]{1,0:T(8,128)(2,1)S(1)}, bf16[64,256]{1,0:T(8,128)(2,1)}, u32[]{:S(2)}) copy-start(bf16[64,256]{1,0:T(8,128)(2,1)} %param.14) | copy-start | bytes 98308
  371.4 322.7 %copy-start.9 = (pred[1024]{0:T(1024)(128)(4,1)S(1)}, pred[1024]{0:T(1024)(128)(4,1)}, u32[]{:S(2)}) copy-start(pred[1024]{0:T(1024)(128)(4,1)} %compare_and_fusion.1) | copy-start | bytes 3076
  604.3 183.1 %copy-start.1 = (bf16[256,192]{0,1:T(8,128)(2,1)S(1)}, bf16[256,192]{0,1:T(8,128)(2,1)}, u32[]{:S(2)}) copy-start(bf16[256,192]{0,1:T(8,128)(2,1)} %param.13) | copy-start | bytes 294916
Sparse Core Ops, SparseCore 0:
  58.1 32.3 reduce-scatter.2
  695.4 91.9 reduce-scatter.4
where the time goes:
time: 798 us; the launch traced here: 794 us
  local copies, waits for them, and re-layouts  410 us (51%)
  waiting for transfers between devices  116 us (15%)
  blocking collectives  111 us (14%)
  matrix products  108 us (14%)
  other arithmetic  23.8 us (3%)
  between operations  15 us (2%)
  starting transfers between devices  9.1 us (1%)
    another operation x21, local copies, waits for them, and re-layouts  138 us
    gather x7, local copies, waits for them, and re-layouts, score_block(): key_pool[page_ids].reshape(req_count, block_len, heads_here, HEAD_DIM)  110 us
    gather x7, local copies, waits for them, and re-layouts, value_block(): value_pool[page_ids].reshape(req_count, block_len, heads_here, HEAD_DIM)  110 us
    reduce_scatter x1, waiting for transfers between devices, on_device(): lax.psum_scatter(jnp.dot(jnp.take(mixed_all, chosen, axis=0), w_out, pref...  92.1 us
    all_gather x1, blocking collectives, on_device(): mixed_all = lax.all_gather(mixed, 'row', axis=0, tiled=True)  85.5 us
    dot_general x7, matrix products, score_block(): jnp.einsum('rhe,rthe->rht', query, keys, preferred_element_type=jnp.float32)  56.5 us
    dot_general x7, matrix products, value_block(): jnp.einsum('rht,rthe->rhe', weights, values, preferred_element_type=jnp.f...  49.4 us
    all_gather x1, blocking collectives, on_device(): gathered = lax.all_gather(xn, 'col', axis=0, tiled=True)  25.9 us
  transfers between devices with their start and end apart: 3, of which 2 were waited for; matrix products, arithmetic and copies ran while one was open for 2% of the time, Pallas kernels for 0%

commit v1 on v0

v1 whole, which is shorter than its diff:
```python
import functools

import jax
import jax.numpy as jnp
import numpy as np
from jax import lax
from jax.experimental import pallas as pl
from jax.experimental.pallas import tpu as pltpu
from jax.sharding import PartitionSpec as P

MESH = pl.DeviceIdType.MESH
BF = jnp.bfloat16
F32 = jnp.float32
HD = 64
PAGE = 64
CHUNK = 16
THETA = 130000.0
MASKED = -1e30
START = -1e20

NN = (((1,), (0,)), ((), ()))
NT = (((1,), (1,)), ((), ()))


def dot(a, b, dims=NN):
    return lax.dot_general(a, b, dims, preferred_element_type=F32)


def iota(shape, dim):
    return lax.broadcasted_iota(jnp.int32, shape, dim)


def kernel(
    rows, cols,
    xn_ref, wqkv_ref, wout_ref, pool_ref, table_ref, lens_ref, freq_ref, deal_ref, mig_ref,
    att_ref, landed_ref,
    kv, vt, g, xall, wall, sq, rq, skv, rkv, ms, mr, ps, pr, lc0, lc1, rl, tt, mx, mxs, mxr, qpad,
    loc_sem, x_sem, w_sem, q_sem, kv_sem, ring_send, ring_recv, m_sem, a_sem,
):
    me_r = lax.axis_index("row")
    me_c = lax.axis_index("col")
    pages = pool_ref.shape[0]
    slots = landed_ref.shape[0]
    all_pages = pages + slots
    reqs = lens_ref.shape[1]
    total = deal_ref.shape[0] * deal_ref.shape[1]
    slot_rows = xn_ref.shape[0]
    half_slots = slots // 2
    far = rows // 2

    pool_copy = pltpu.make_async_copy(pool_ref, kv.at[pl.ds(0, pages)], loc_sem.at[0])
    pool_copy.start()

    barrier = pltpu.get_barrier_semaphore()

    def greet_col(o, carry):
        pl.semaphore_signal(barrier, inc=1, device_id={"col": lax.rem(me_c + o, cols)}, device_id_type=MESH)
        return carry

    def greet_row(o, carry):
        pl.semaphore_signal(barrier, inc=1, device_id={"row": lax.rem(me_r + o, rows)}, device_id_type=MESH)
        return carry

    lax.fori_loop(1, cols, greet_col, 0)
    lax.fori_loop(1, rows, greet_row, 0)
    pl.semaphore_wait(barrier, cols + rows - 2)

    def to_cols(src, dst, sems):
        def send(o, carry):
            to = lax.rem(me_c + o, cols)
            pltpu.make_async_remote_copy(
                src_ref=src(to), dst_ref=dst, send_sem=sems.at[0], recv_sem=sems.at[1],
                device_id={"col": to}, device_id_type=MESH,
            ).start()
            return carry
        lax.fori_loop(1, cols, send, 0)

    def to_rows(src, dst, sems):
        def send(o, carry):
            to = lax.rem(me_r + o, rows)
            pltpu.make_async_remote_copy(
                src_ref=src(to), dst_ref=dst, send_sem=sems.at[0], recv_sem=sems.at[1],
                device_id={"row": to}, device_id_type=MESH,
            ).start()
            return carry
        lax.fori_loop(1, rows, send, 0)

    def wait_all(buf, count, sem):
        part = buf.at[pl.ds(0, count)]
        pltpu.make_async_copy(part, part, sem).wait()

    to_cols(lambda to: xn_ref, xall.at[me_c], x_sem)
    xall[me_c] = xn_ref[...]
    to_cols(lambda to: wout_ref, wall.at[me_c], w_sem)
    wall[me_c] = wout_ref[...]

    left = lax.rem(me_r + rows - 1, rows)
    right = lax.rem(me_r + 1, rows)

    def ring_step(step):
        for sign, out, came, to in ((0, ms, mr, left), (1, ps, pr, right)):
            dist = far - step
            block = lax.rem(me_r + (rows - dist if sign == 0 else dist), rows)
            lead = 0 if sign == 0 else half_slots
            first, count = (lead, half_slots) if step == 0 else (0, slots)

            def fill(t, carry):
                src = mig_ref[block * slots + t]
                own = src // pages == me_r
                page = kv[src % pages]
                out[step, t] = page if step == 0 else jnp.where(own, page, came[step - 1, t])
                return carry

            def begin(t, carry):
                out[step, t] = kv[mig_ref[block * slots + t] % pages]
                return carry

            if step == 1:
                lax.fori_loop(lead, lead + half_slots, fill, 0)
                lax.fori_loop(half_slots - lead, slots - lead, begin, 0)
            else:
                lax.fori_loop(first, first + count, fill, 0)
            ring_copy(sign, step).start()

    def ring_copy(sign, step):
        out, came, to = (ms, mr, left) if sign == 0 else (ps, pr, right)
        lead = 0 if sign == 0 else half_slots
        part = pl.ds(lead, half_slots) if step == 0 else pl.ds(0, slots)
        return pltpu.make_async_remote_copy(
            src_ref=out.at[step, part], dst_ref=came.at[step, part],
            send_sem=ring_send.at[sign, step], recv_sem=ring_recv.at[sign, step],
            device_id={"row": to}, device_id_type=MESH,
        )

    def ring_arrive(step):
        for sign in (0, 1):
            ring_copy(sign, step).wait_recv()

    pool_copy.wait()
    ring_step(0)

    lens = lens_ref[...]
    full = lens // PAGE
    rest = (lens - full * PAGE).astype(F32)
    entries = table_ref.shape[1]
    wide = jnp.concatenate(
        [table_ref[...].astype(F32), jnp.zeros((reqs, reqs - entries), F32)], axis=1
    ) if entries < reqs else table_ref[...].astype(F32)
    turned = wide.T[:entries]
    at = iota((entries, reqs), 0)
    tt[...] = jnp.where(at < full, turned, -1.0)
    last = jnp.max(jnp.where(at == full, turned, -1.0), axis=0, keepdims=True)
    halves = 2
    per = all_pages // halves
    for part in range(halves):
        ids = (iota((per, reqs), 0) + part * per).astype(F32)

        def tally(t, count):
            return count + jnp.where(tt[pl.ds(t, 1), :] == ids, 1.0, 0.0)

        count = lax.fori_loop(0, entries, tally, jnp.zeros((per, reqs), F32))
        where = pl.ds(part * per, per)
        lc0[where, :] = jnp.where(count > 0.0, jnp.log(jnp.maximum(count, 1.0)), MASKED)
        lc1[where, :] = jnp.log(count + 1.0)
        rl[where, :] = jnp.where(last == ids, rest, 0.0)

    lanes = iota((128, 128), 1).astype(F32)
    for jb in range(total // 128):
        column = jnp.broadcast_to(deal_ref[jb : jb + 1, :].astype(F32), (128, 128)).T
        for ib in range(total // 128):
            g[jb * 128 : jb * 128 + 128, ib * 128 : ib * 128 + 128] = jnp.where(
                column == lanes + float(ib * 128), 1.0, 0.0
            ).astype(BF)

    angles = freq_ref[...] * lens.astype(F32)
    cosine = jnp.cos(angles)
    sine = jnp.sin(angles)

    width = wqkv_ref.shape[1]
    eye = jnp.where(iota((width, width), 0) == iota((width, width), 1), 1.0, 0.0).astype(BF)
    w_turned = dot(eye, wqkv_ref[...], NT).astype(BF)

    pick = jnp.where(iota((HD, 2 * HD), 0) + HD == iota((HD, 2 * HD), 1), 1.0, 0.0).astype(BF)

    def turn(c, carry):
        tokens = kv[pl.ds(c * CHUNK, CHUNK)].reshape(CHUNK * PAGE, 2 * HD)
        vt[c] = dot(pick, tokens, NT).astype(BF)
        return carry

    lax.fori_loop(0, pages // CHUNK, turn, 0)

    wait_all(xall, cols - 1, x_sem.at[1])
    projected = dot(w_turned, xall[...].reshape(total, xn_ref.shape[1]), NT).astype(BF)
    for b in range(rows):
        block = dot(projected, g[:, b * reqs : (b + 1) * reqs]).astype(BF)
        sq[b] = block[:HD]
        skv[b] = block[HD:]
    to_rows(lambda to: sq.at[to], rq.at[me_r], q_sem)
    to_rows(lambda to: skv.at[to], rkv.at[me_r], kv_sem)

    ring_arrive(0)
    ring_step(1)

    def rotate(x):
        u, w = x[: HD // 2], x[HD // 2 :]
        return jnp.concatenate([u * cosine - w * sine, w * cosine + u * sine], axis=0).astype(BF)

    wait_all(rq, rows - 1, q_sem.at[1])
    summed = sq[me_r].astype(F32)
    for o in range(1, rows):
        summed = summed + rq[lax.rem(me_r + o, rows)].astype(F32)
    query = rotate(summed)
    qpad[...] = jnp.concatenate([query * jnp.asarray(0.125, BF), jnp.zeros((HD, reqs), BF)], axis=0)

    offsets = iota((PAGE, reqs), 0).astype(F32)

    def chunk(c, carry):
        top, norm, acc = carry
        tokens = kv[pl.ds(c * CHUNK, CHUNK)].reshape(CHUNK * PAGE, 2 * HD)
        raw = dot(tokens, qpad[...])
        scores = []
        for p in range(CHUNK):
            row = pl.ds(c * CHUNK + p, 1)
            bias = jnp.where(offsets < rl[row, :], lc1[row, :], lc0[row, :])
            scores.append(raw[p * PAGE : (p + 1) * PAGE] + bias)
        scores = jnp.concatenate(scores, axis=0)
        new_top = jnp.maximum(top, jnp.max(scores, axis=0, keepdims=True))
        weights = jnp.exp(scores - new_top)
        scale = jnp.exp(top - new_top)
        norm = norm * scale + jnp.sum(weights, axis=0, keepdims=True)
        acc = acc * scale + dot(vt[c], weights.astype(BF))
        return new_top, norm, acc

    carry = (jnp.full((1, reqs), START, F32), jnp.zeros((1, reqs), F32), jnp.zeros((HD, reqs), F32))
    chunks = pages // CHUNK
    carry = lax.fori_loop(0, chunks // 2, chunk, carry)
    ring_arrive(1)
    ring_step(2)
    carry = lax.fori_loop(chunks // 2, chunks, chunk, carry)

    wait_all(rkv, rows - 1, kv_sem.at[1])
    summed = skv[me_r].astype(F32)
    for o in range(1, rows):
        summed = summed + rkv[lax.rem(me_r + o, rows)].astype(F32)
    key_new = rotate(summed[:HD])
    value_new = summed[HD:].astype(BF)

    ring_arrive(2)
    ring_step(3)

    top, norm, acc = carry
    score_new = jnp.sum(query.astype(F32) * key_new.astype(F32), axis=0, keepdims=True) * 0.125
    new_top = jnp.maximum(top, score_new)
    scale = jnp.exp(top - new_top)
    weight_new = jnp.exp(score_new - new_top)
    norm = norm * scale + weight_new
    acc = acc * scale + weight_new.astype(BF).astype(F32) * value_new.astype(F32)

    ring_arrive(3)

    def settle(t, carry):
        src = mig_ref[me_r * slots + t] // pages
        away = lax.rem(src - me_r + rows, rows)
        low = jnp.logical_or(away < far, jnp.logical_and(away == far, t < half_slots))
        kv[pages + t] = jnp.where(low, mr[far - 1, t], pr[far - 1, t])
        return carry

    lax.fori_loop(0, slots, settle, 0)
    landed_copy = pltpu.make_async_copy(kv.at[pl.ds(pages, slots)], landed_ref, loc_sem.at[1])
    landed_copy.start()
    turn(chunks, 0)
    top, norm, acc = chunk(chunks, (new_top, norm, acc))
    mixed = (acc / norm).astype(BF)

    mx[me_r] = mixed
    to_rows(lambda to: mx.at[me_r], mx.at[me_r], m_sem)
    wait_all(mx, rows - 1, m_sem.at[1])
    heads = jnp.concatenate([mx[b] for b in range(rows)], axis=1)
    odd = lax.rem(me_c, 2)
    none = jnp.zeros_like(heads)
    placed = jnp.concatenate(
        [jnp.where(odd == 0, heads, none), jnp.where(odd == 0, none, heads)], axis=0
    )
    mxs[...] = dot(g[...], placed, NT).astype(BF).reshape(mxs.shape)
    to_cols(lambda to: mxs.at[to], mxr.at[me_c], a_sem)
    mxr[me_c] = mxs[me_c]
    wait_all(wall, cols - 1, w_sem.at[1])
    wait_all(mxr, cols - 1, a_sem.at[1])
    pairs = jnp.concatenate([mxr[2 * k] + mxr[2 * k + 1] for k in range(cols // 2)], axis=1)
    att_ref[...] = dot(pairs, wall[...].reshape(cols * HD, wout_ref.shape[1])).astype(BF)

    wait_all(xall, cols - 1, x_sem.at[0])
    wait_all(wall, cols - 1, w_sem.at[0])
    wait_all(rq, rows - 1, q_sem.at[0])
    wait_all(rkv, rows - 1, kv_sem.at[0])
    wait_all(mx, rows - 1, m_sem.at[0])
    wait_all(mxr, cols - 1, a_sem.at[0])
    for step in range(far):
        for sign in (0, 1):
            ring_copy(sign, step).wait_send()
    landed_copy.wait()


def on_device(rows, cols, interpret, xn, w_qkv, w_out, pool, page_table, lengths, mig_src, deal):
    reqs = lengths.shape[0]
    pages, page, lanes = pool.shape
    slots = mig_src.shape[0] // rows
    total = deal.shape[0]
    slot_rows, depth = xn.shape
    freqs = THETA ** (-(np.arange(HD // 2, dtype=np.float64) * 2.0 / HD))
    freqs = jnp.asarray(np.repeat(freqs.astype(np.float32)[:, None], reqs, axis=1))
    vmem = pl.BlockSpec(memory_space=pltpu.VMEM)
    hbm = pl.BlockSpec(memory_space=pl.ANY)
    smem = pl.BlockSpec(memory_space=pltpu.SMEM)
    far = rows // 2
    dma = pltpu.SemaphoreType.DMA
    return pl.pallas_call(
        functools.partial(kernel, rows, cols),
        out_shape=(
            jax.ShapeDtypeStruct((slot_rows, w_out.shape[1]), BF),
            jax.ShapeDtypeStruct((slots, page, lanes), BF),
        ),
        in_specs=[vmem, vmem, vmem, hbm, vmem, vmem, vmem, vmem, smem],
        out_specs=(vmem, hbm),
        scratch_shapes=[
            pltpu.VMEM((pages + slots, page, lanes), BF),
            pltpu.VMEM(((pages + slots) // CHUNK, HD, CHUNK * page), BF),
            pltpu.VMEM((total, total), BF),
            pltpu.VMEM((cols, slot_rows, depth), BF),
            pltpu.VMEM((cols, HD, w_out.shape[1]), BF),
            pltpu.VMEM((rows, HD, reqs), BF),
            pltpu.VMEM((rows, HD, reqs), BF),
            pltpu.VMEM((rows, 2 * HD, reqs), BF),
            pltpu.VMEM((rows, 2 * HD, reqs), BF),
            pltpu.VMEM((far, slots, page, lanes), BF),
            pltpu.VMEM((far, slots, page, lanes), BF),
            pltpu.VMEM((far, slots, page, lanes), BF),
            pltpu.VMEM((far, slots, page, lanes), BF),
            pltpu.VMEM((pages + slots, reqs), F32),
            pltpu.VMEM((pages + slots, reqs), F32),
            pltpu.VMEM((pages + slots, reqs), F32),
            pltpu.VMEM((page_table.shape[1], reqs), F32),
            pltpu.VMEM((rows, HD, reqs), BF),
            pltpu.VMEM((cols, slot_rows, 2 * HD), BF),
            pltpu.VMEM((cols, slot_rows, 2 * HD), BF),
            pltpu.VMEM((2 * HD, reqs), BF),
            dma((2,)), dma((2,)), dma((2,)), dma((2,)), dma((2,)),
            dma((2, far)), dma((2, far)), dma((2,)), dma((2,)),
        ],
        compiler_params=pltpu.CompilerParams(
            collective_id=0, has_side_effects=True, vmem_limit_bytes=50 * 2**20
        ),
    )(xn, w_qkv, w_out, pool, page_table, lengths.reshape(1, reqs), freqs, deal.reshape(total // 128, 128), mig_src)


def solution(mesh):
    return jax.shard_map(
        functools.partial(on_device, mesh.shape["row"], mesh.shape["col"], False),
        mesh=mesh,
        in_specs=(
            P("col", "row"),
            P("row", "col"),
            P("col", "row"),
            P("row", None, "col"),
            P("row", None),
            P("row"),
            P(),
            P(),
        ),
        out_specs=(P("col", "row"), P("row", None, "col")),
        check_vma=False,
    )
```

time: 798 us -> 84.5 us (0.11)
  local copies, waits for them, and re-layouts: 410 us -> 7.34 us
  waiting for transfers between devices: 116 us -> 0 us
  blocking collectives: 111 us -> 0 us
  matrix products: 108 us -> 0 us
  Pallas kernels: 0 us -> 76.1 us
  other arithmetic: 23.8 us -> 0 us
  between operations: 15 us -> 0.66 us
  starting transfers between devices: 9.1 us -> 0 us
    gather x19 -> x0, local copies, waits for them, and re-layouts: 232 us -> none  [the longest x7 110 us: score_block(): key_pool[page_ids].reshape(req_count, block_len, heads_here, HEAD_DIM)]
    another operation x21 -> x0, local copies, waits for them, and re-layouts: 138 us -> none
    reduce_scatter x2 -> x0, waiting for transfers between devices: 116 us -> none  [the longest x1 92.1 us: on_device(): lax.psum_scatter(jnp.dot(jnp.take(mixed_all, chosen, axis=0), w_out, pref...]
    all_gather x2 -> x0, blocking collectives: 111 us -> none  [the longest x1 85.5 us: on_device(): mixed_all = lax.all_gather(mixed, 'row', axis=0, tiled=True)]
    dot_general x16 -> x0, matrix products: 108 us -> none  [the longest x7 56.5 us: score_block(): jnp.einsum('rhe,rthe->rht', query, keys, preferred_element_type=jnp.float32)]
    pallas_call x0 -> x1, Pallas kernels: none -> 76.1 us  [on_device(): pl.pallas_call(functools.partial(kernel, rows, cols), out_shape=(jax.Shap...]
    dynamic_update_slice x7 -> x0, local copies, waits for them, and re-layouts: 13.1 us -> none  [score_block(): lax.dynamic_update_slice_in_dim(scores, block_scores, block_no * block_le...]
    all_to_all x1 -> x0, starting transfers between devices: 9.01 us -> none  [on_device(): lax.all_to_all(outgoing, 'row', split_axis=0, concat_axis=0, tiled=True)]
  transfers between devices with their start and end apart: 3 -> 0, of which waited for: 2 -> 0; matrix products, arithmetic and copies ran while one was open for 2% -> 0% of each run, Pallas kernels for 0% -> 0%
where the time goes in v1:
time: 84.5 us; the launch traced here: 84.1 us
  Pallas kernels  76.1 us (90%)
  local copies, waits for them, and re-layouts  7.34 us (9%)
    pallas_call x1, Pallas kernels, on_device(): pl.pallas_call(functools.partial(kernel, rows, cols), out_shape=(jax.Shap...  76.1 us
    unnamed x16, local copies, waits for them, and re-layouts  7.34 us

profile of v1, /device:TPU:1, one launch (start us, length us, event | category | flops | bytes accessed | tf_op | source)
XLA Modules:
  0.0 84.1 jit_solution(2441096747794378026)
XLA Ops:
  0.6 0.8 %copy.12.table_ref = s32[128,64]{1,0:T(8,128)S(1)} copy(s32[128,64]{0,1:T(8,128)} %param.13) | data formatting | bytes 65536 | tf_op args[4]
  1.5 1.0 %copy.11.wqkv_ref = bf16[256,192]{1,0:T(8,128)(2,1)S(1)} copy(bf16[256,192]{0,1:T(8,128)(2,1)} %param.10) | data formatting | bytes 196608 | tf_op args[1]
  2.5 0.0 copy-start
  2.5 0.7 copy-done
  3.2 0.0 copy-start.1
  3.2 0.7 copy-done.1
  4.0 0.0 copy-start.2
  4.0 0.7 copy-done.2
  4.7 0.0 copy-start.3
  4.7 0.7 copy-done.3
  5.4 0.0 copy-start.4
  5.4 0.7 copy-done.4
  6.0 0.0 copy-start.5
  6.0 0.7 copy-done.5
  6.7 76.1 %shard_map.104 = (bf16[32,256]{1,0:T(8,128)(2,1)S(1)}, bf16[16,64,128]{2,1,0:T(8,128)(2,1)S(1)}) custom-call(bf16[32,256]{1,0:T(8,128)(2,1)S(1)} %copy-done.1, bf16[256,192]{1,0:T(8,128)(2,1)S(1)} %copy.11.wqkv_ref, bf16[64,256]{1,0:T(8,128)(2,1)S(1)} %copy-done, bf16[256,64,128]{2,1,0:T(8,128)(2,1)} %pool_ref.1, s32[128,64]{1,0:T(8,128)S(1)} %copy.12.table_ref, ...), custom_call_target="tpu_custom_call" | custom-call | tf_op jit(solution)/shard_map/pallas_call | solution.py:317
  82.8 0.6 copy.15
  83.4 0.7 copy.16
Async XLA Ops:
  2.5 0.8 copy-start
  3.2 0.7 copy-start.1
  4.0 0.7 copy-start.2
  4.7 0.7 copy-start.3
  5.4 0.7 copy-start.4
  6.0 0.7 copy-start.5

commit v2 on v1

--- a/solution.py
+++ b/solution.py
@@ -32,9 +32,9 @@
 
 def kernel(
     rows, cols,
-    xn_ref, wqkv_ref, wout_ref, pool_ref, table_ref, lens_ref, freq_ref, deal_ref, mig_ref,
+    xn_ref, wqkv_hbm, wout_ref, pool_ref, table_hbm, lens_hbm, freq_hbm, deal_hbm, mig_hbm,
     att_ref, landed_ref,
-    kv, vt, g, xall, wall, sq, rq, skv, rkv, ms, mr, ps, pr, lc0, lc1, rl, tt, mx, mxs, mxr, qpad,
+    wqkv_ref, table_ref, lens_ref, freq_ref, deal_ref, mig_ref, kv, vt, g, xall, wall, sq, rq, skv, rkv, ms, mr, ps, pr, lc0, lc1, rl, tt, mx, mxs, mxr, qpad,
     loc_sem, x_sem, w_sem, q_sem, kv_sem, ring_send, ring_recv, m_sem, a_sem,
 ):
     me_r = lax.axis_index("row")
@@ -48,8 +48,26 @@
     half_slots = slots // 2
     far = rows // 2
 
-    pool_copy = pltpu.make_async_copy(pool_ref, kv.at[pl.ds(0, pages)], loc_sem.at[0])
-    pool_copy.start()
+    parts = 4
+    pool_copies = [
+        pltpu.make_async_copy(
+            pool_ref.at[pl.ds(n * (pages // parts), pages // parts)],
+            kv.at[pl.ds(n * (pages // parts), pages // parts)],
+            loc_sem.at[10 + n],
+        )
+        for n in range(parts)
+    ]
+    small = [
+        pltpu.make_async_copy(src, dst, loc_sem.at[2 + n])
+        for n, (src, dst) in enumerate((
+            (mig_hbm, mig_ref), (lens_hbm, lens_ref), (table_hbm, table_ref), (deal_hbm, deal_ref),
+            (freq_hbm, freq_ref), (wqkv_hbm, wqkv_ref), (xn_ref, xall.at[me_c]), (wout_ref, wall.at[me_c]),
+        ))
+    ]
+    for copy in small:
+        copy.start()
+    for copy in pool_copies:
+        copy.start()
 
     barrier = pltpu.get_barrier_semaphore()
 
@@ -90,63 +108,67 @@
         pltpu.make_async_copy(part, part, sem).wait()
 
     to_cols(lambda to: xn_ref, xall.at[me_c], x_sem)
-    xall[me_c] = xn_ref[...]
-    to_cols(lambda to: wout_ref, wall.at[me_c], w_sem)
-    wall[me_c] = wout_ref[...]
 
     left = lax.rem(me_r + rows - 1, rows)
     right = lax.rem(me_r + 1, rows)
 
-    def ring_step(step):
-        for sign, out, came, to in ((0, ms, mr, left), (1, ps, pr, right)):
-            dist = far - step
-            block = lax.rem(me_r + (rows - dist if sign == 0 else dist), rows)
-            lead = 0 if sign == 0 else half_slots
-            first, count = (lead, half_slots) if step == 0 else (0, slots)
-
-            def fill(t, carry):
-                src = mig_ref[block * slots + t]
-                own = src // pages == me_r
-                page = kv[src % pages]
-                out[step, t] = page if step == 0 else jnp.where(own, page, came[step - 1, t])
-                return carry
-
-            def begin(t, carry):
-                out[step, t] = kv[mig_ref[block * slots + t] % pages]
-                return carry
-
-            if step == 1:
-                lax.fori_loop(lead, lead + half_slots, fill, 0)
-                lax.fori_loop(half_slots - lead, slots - lead, begin, 0)
-            else:
-                lax.fori_loop(first, first + count, fill, 0)
-            ring_copy(sign, step).start()
-
-    def ring_copy(sign, step):
+    def hops(sign, half):
+        return far if sign == half else far - 1
+
+    def ring_copy(sign, half, hop):
         out, came, to = (ms, mr, left) if sign == 0 else (ps, pr, right)
-        lead = 0 if sign == 0 else half_slots
-        part = pl.ds(lead, half_slots) if step == 0 else pl.ds(0, slots)
         return pltpu.make_async_remote_copy(
-            src_ref=out.at[step, part], dst_ref=came.at[step, part],
-            send_sem=ring_send.at[sign, step], recv_sem=ring_recv.at[sign, step],
+            src_ref=out.at[half, hop], dst_ref=came.at[half, hop],
+            send_sem=ring_send.at[sign, half, hop], recv_sem=ring_recv.at[sign, half, hop],
             device_id={"row": to}, device_id_type=MESH,
         )
 
-    def ring_arrive(step):
+    def ring_hop(hop, long):
         for sign in (0, 1):
-            ring_copy(sign, step).wait_recv()
-
-    pool_copy.wait()
-    ring_step(0)
+            half = sign if long else 1 - sign
+            out, came = (ms, mr) if sign == 0 else (ps, pr)
+            dist = hops(sign, half) - hop
+            block = lax.rem(me_r + (rows - dist if sign == 0 else dist), rows)
+            first = block * slots + half * half_slots
+            if hop > 0:
+                ring_copy(sign, half, hop - 1).wait_recv()
+
+            def fill(t, carry):
+                src = mig_ref[first + t]
+                page = kv[src % pages]
+                if hop > 0:
+                    page = jnp.where(src // pages == me_r, page, came[half, hop - 1, t])
+                out[half, hop, t] = page
+                return carry
+
+            lax.fori_loop(0, half_slots, fill, 0)
+            ring_copy(sign, half, hop).start()
+
+    for copy in small:
+        copy.wait()
+    for copy in pool_copies:
+        copy.wait()
+    ring_hop(0, True)
+    ring_hop(0, False)
 
     lens = lens_ref[...]
+
+    lanes = iota((128, 128), 1).astype(F32)
+    for jb in range(total // 128):
+        column = jnp.broadcast_to(deal_ref[jb : jb + 1, :].astype(F32), (128, 128)).T
+        for ib in range(total // 128):
+            g[jb * 128 : jb * 128 + 128, ib * 128 : ib * 128 + 128] = jnp.where(
+                column == lanes + float(ib * 128), 1.0, 0.0
+            ).astype(BF)
+
+    angles = freq_ref[...] * lens.astype(F32)
+    cosine = jnp.cos(angles)
+    sine = jnp.sin(angles)
+
     full = lens // PAGE
     rest = (lens - full * PAGE).astype(F32)
-    entries = table_ref.shape[1]
-    wide = jnp.concatenate(
-        [table_ref[...].astype(F32), jnp.zeros((reqs, reqs - entries), F32)], axis=1
-    ) if entries < reqs else table_ref[...].astype(F32)
-    turned = wide.T[:entries]
+    entries = table_ref.shape[0]
+    turned = table_ref[...].astype(F32)
     at = iota((entries, reqs), 0)
     tt[...] = jnp.where(at < full, turned, -1.0)
     last = jnp.max(jnp.where(at == full, turned, -1.0), axis=0, keepdims=True)
@@ -164,21 +186,7 @@
         lc1[where, :] = jnp.log(count + 1.0)
         rl[where, :] = jnp.where(last == ids, rest, 0.0)
 
-    lanes = iota((128, 128), 1).astype(F32)
-    for jb in range(total // 128):
-        column = jnp.broadcast_to(deal_ref[jb : jb + 1, :].astype(F32), (128, 128)).T
-        for ib in range(total // 128):
-            g[jb * 128 : jb * 128 + 128, ib * 128 : ib * 128 + 128] = jnp.where(
-                column == lanes + float(ib * 128), 1.0, 0.0
-            ).astype(BF)
-
-    angles = freq_ref[...] * lens.astype(F32)
-    cosine = jnp.cos(angles)
-    sine = jnp.sin(angles)
-
-    width = wqkv_ref.shape[1]
-    eye = jnp.where(iota((width, width), 0) == iota((width, width), 1), 1.0, 0.0).astype(BF)
-    w_turned = dot(eye, wqkv_ref[...], NT).astype(BF)
+    ring_hop(1, True)
 
     pick = jnp.where(iota((HD, 2 * HD), 0) + HD == iota((HD, 2 * HD), 1), 1.0, 0.0).astype(BF)
 
@@ -190,7 +198,7 @@
     lax.fori_loop(0, pages // CHUNK, turn, 0)
 
     wait_all(xall, cols - 1, x_sem.at[1])
-    projected = dot(w_turned, xall[...].reshape(total, xn_ref.shape[1]), NT).astype(BF)
+    projected = dot(wqkv_ref[...], xall[...].reshape(total, xn_ref.shape[1]), NT).astype(BF)
     for b in range(rows):
         block = dot(projected, g[:, b * reqs : (b + 1) * reqs]).astype(BF)
         sq[b] = block[:HD]
@@ -198,8 +206,8 @@
     to_rows(lambda to: sq.at[to], rq.at[me_r], q_sem)
     to_rows(lambda to: skv.at[to], rkv.at[me_r], kv_sem)
 
-    ring_arrive(0)
-    ring_step(1)
+    ring_hop(1, False)
+    to_cols(lambda to: wout_ref, wall.at[me_c], w_sem)
 
     def rotate(x):
         u, w = x[: HD // 2], x[HD // 2 :]
@@ -233,9 +241,9 @@
 
     carry = (jnp.full((1, reqs), START, F32), jnp.zeros((1, reqs), F32), jnp.zeros((HD, reqs), F32))
     chunks = pages // CHUNK
+    ring_hop(2, True)
     carry = lax.fori_loop(0, chunks // 2, chunk, carry)
-    ring_arrive(1)
-    ring_step(2)
+    ring_hop(2, False)
     carry = lax.fori_loop(chunks // 2, chunks, chunk, carry)
 
     wait_all(rkv, rows - 1, kv_sem.at[1])
@@ -245,8 +253,7 @@
     key_new = rotate(summed[:HD])
     value_new = summed[HD:].astype(BF)
 
-    ring_arrive(2)
-    ring_step(3)
+    ring_hop(3, True)
 
     top, norm, acc = carry
     score_new = jnp.sum(query.astype(F32) * key_new.astype(F32), axis=0, keepdims=True) * 0.125
@@ -256,16 +263,22 @@
     norm = norm * scale + weight_new
     acc = acc * scale + weight_new.astype(BF).astype(F32) * value_new.astype(F32)
 
-    ring_arrive(3)
-
-    def settle(t, carry):
-        src = mig_ref[me_r * slots + t] // pages
-        away = lax.rem(src - me_r + rows, rows)
-        low = jnp.logical_or(away < far, jnp.logical_and(away == far, t < half_slots))
-        kv[pages + t] = jnp.where(low, mr[far - 1, t], pr[far - 1, t])
-        return carry
-
-    lax.fori_loop(0, slots, settle, 0)
+    for half in (1, 0):
+        for sign in (0, 1):
+            side = half if sign == 0 else 1 - half
+            ring_copy(sign, side, hops(sign, side) - 1).wait_recv()
+
+    for half in (0, 1):
+        def settle(t, carry):
+            src = mig_ref[me_r * slots + half * half_slots + t] // pages
+            away = lax.rem(src - me_r + rows, rows)
+            low = away <= far if half == 0 else away < far
+            kv[pages + half * half_slots + t] = jnp.where(
+                low, mr[half, hops(0, half) - 1, t], pr[half, hops(1, half) - 1, t]
+            )
+            return carry
+
+        lax.fori_loop(0, half_slots, settle, 0)
     landed_copy = pltpu.make_async_copy(kv.at[pl.ds(pages, slots)], landed_ref, loc_sem.at[1])
     landed_copy.start()
     turn(chunks, 0)
@@ -295,9 +308,10 @@
     wait_all(rkv, rows - 1, kv_sem.at[0])
     wait_all(mx, rows - 1, m_sem.at[0])
     wait_all(mxr, cols - 1, a_sem.at[0])
-    for step in range(far):
-        for sign in (0, 1):
-            ring_copy(sign, step).wait_send()
+    for sign in (0, 1):
+        for half in (0, 1):
+            for hop in range(hops(sign, half)):
+                ring_copy(sign, half, hop).wait_send()
     landed_copy.wait()
 
 
@@ -310,8 +324,7 @@
     freqs = THETA ** (-(np.arange(HD // 2, dtype=np.float64) * 2.0 / HD))
     freqs = jnp.asarray(np.repeat(freqs.astype(np.float32)[:, None], reqs, axis=1))
     vmem = pl.BlockSpec(memory_space=pltpu.VMEM)
-    hbm = pl.BlockSpec(memory_space=pl.ANY)
-    smem = pl.BlockSpec(memory_space=pltpu.SMEM)
+    hbm = pl.BlockSpec(memory_space=pltpu.HBM)
     far = rows // 2
     dma = pltpu.SemaphoreType.DMA
     return pl.pallas_call(
@@ -320,9 +333,15 @@
             jax.ShapeDtypeStruct((slot_rows, w_out.shape[1]), BF),
             jax.ShapeDtypeStruct((slots, page, lanes), BF),
         ),
-        in_specs=[vmem, vmem, vmem, hbm, vmem, vmem, vmem, vmem, smem],
-        out_specs=(vmem, hbm),
+        in_specs=[hbm] * 9,
+        out_specs=(vmem, pl.BlockSpec(memory_space=pl.ANY)),
         scratch_shapes=[
+            pltpu.VMEM((w_qkv.shape[1], depth), BF),
+            pltpu.VMEM((page_table.shape[1], reqs), jnp.int32),
+            pltpu.VMEM((1, reqs), jnp.int32),
+            pltpu.VMEM((HD // 2, reqs), F32),
+            pltpu.VMEM((total // 128, 128), jnp.int32),
+            pltpu.SMEM(mig_src.shape, jnp.int32),
             pltpu.VMEM((pages + slots, page, lanes), BF),
             pltpu.VMEM(((pages + slots) // CHUNK, HD, CHUNK * page), BF),
             pltpu.VMEM((total, total), BF),
@@ -332,10 +351,10 @@
             pltpu.VMEM((rows, HD, reqs), BF),
             pltpu.VMEM((rows, 2 * HD, reqs), BF),
             pltpu.VMEM((rows, 2 * HD, reqs), BF),
-            pltpu.VMEM((far, slots, page, lanes), BF),
-            pltpu.VMEM((far, slots, page, lanes), BF),
-            pltpu.VMEM((far, slots, page, lanes), BF),
-            pltpu.VMEM((far, slots, page, lanes), BF),
+            pltpu.VMEM((2, far, slots // 2, page, lanes), BF),
+            pltpu.VMEM((2, far, slots // 2, page, lanes), BF),
+            pltpu.VMEM((2, far, slots // 2, page, lanes), BF),
+            pltpu.VMEM((2, far, slots // 2, page, lanes), BF),
             pltpu.VMEM((pages + slots, reqs), F32),
             pltpu.VMEM((pages + slots, reqs), F32),
             pltpu.VMEM((pages + slots, reqs), F32),
@@ -344,13 +363,13 @@
             pltpu.VMEM((cols, slot_rows, 2 * HD), BF),
             pltpu.VMEM((cols, slot_rows, 2 * HD), BF),
             pltpu.VMEM((2 * HD, reqs), BF),
-            dma((2,)), dma((2,)), dma((2,)), dma((2,)), dma((2,)),
-            dma((2, far)), dma((2, far)), dma((2,)), dma((2,)),
+            dma((14,)), dma((2,)), dma((2,)), dma((2,)), dma((2,)),
+            dma((2, 2, far)), dma((2, 2, far)), dma((2,)), dma((2,)),
         ],
         compiler_params=pltpu.CompilerParams(
-            collective_id=0, has_side_effects=True, vmem_limit_bytes=50 * 2**20
+            collective_id=0, has_side_effects=True, vmem_limit_bytes=64 * 2**20
         ),
-    )(xn, w_qkv, w_out, pool, page_table, lengths.reshape(1, reqs), freqs, deal.reshape(total // 128, 128), mig_src)
+    )(xn, w_qkv.T, w_out, pool, page_table.T, lengths.reshape(1, reqs), freqs, deal.reshape(total // 128, 128), mig_src)
 
 
 def solution(mesh):

time: 84.5 us -> 64.4 us (0.76)
  Pallas kernels: 76.1 us -> 60.6 us
  local copies, waits for them, and re-layouts: 7.34 us -> 2.99 us
    pallas_call x1, Pallas kernels: 76.1 us -> 60.6 us  [on_device(): pl.pallas_call(functools.partial(kernel, rows, cols), out_shape=(jax.Shap...]
    unnamed x16 -> x2, local copies, waits for them, and re-layouts: 7.34 us -> 2.99 us
where the time goes in v2:
time: 64.4 us; the launch traced here: 64.2 us
  Pallas kernels  60.6 us (94%)
  local copies, waits for them, and re-layouts  2.99 us (5%)
    pallas_call x1, Pallas kernels, on_device(): pl.pallas_call(functools.partial(kernel, rows, cols), out_shape=(jax.Shap...  60.6 us
    unnamed x2, local copies, waits for them, and re-layouts  2.99 us

profile of v2, /device:TPU:1, one launch (start us, length us, event | category | flops | bytes accessed | tf_op | source)
XLA Modules:
  0.0 64.2 jit_solution(14785795372769444570)
XLA Ops:
  0.6 60.6 %shard_map.104 = (bf16[32,256]{1,0:T(8,128)(2,1)}, bf16[16,64,128]{2,1,0:T(8,128)(2,1)}) custom-call(bf16[32,256]{1,0:T(8,128)(2,1)} %xn_ref.1, bf16[192,256]{1,0:T(8,128)(2,1)} %bitcast.4, bf16[64,256]{1,0:T(8,128)(2,1)} %wout_ref.1, bf16[256,64,128]{2,1,0:T(8,128)(2,1)} %pool_ref.1, s32[64,128]{1,0:T(8,128)} %bitcast.5, s32[1,128]{1,0:T(1,128)} %bitcast.7, ...), custom_call_target="tpu_custom_call" | custom-call | tf_op jit(solution)/shard_map/pallas_call | solution.py:330
  61.2 1.3 %copy.13 = bf16[32,256]{1,0:T(8,128)(2,1)} copy(bf16[32,256]{1,0:T(8,128)(2,1)} %get-tuple-element.4) | data formatting | bytes 32768
  62.5 1.7 %copy.14 = bf16[16,64,128]{2,1,0:T(8,128)(2,1)} copy(bf16[16,64,128]{2,1,0:T(8,128)(2,1)} %get-tuple-element.5) | data formatting | bytes 524288

commit v3 on v2

--- a/solution.py
+++ b/solution.py
@@ -34,8 +34,8 @@
     rows, cols,
     xn_ref, wqkv_hbm, wout_ref, pool_ref, table_hbm, lens_hbm, freq_hbm, deal_hbm, mig_hbm,
     att_ref, landed_ref,
-    wqkv_ref, table_ref, lens_ref, freq_ref, deal_ref, mig_ref, kv, vt, g, xall, wall, sq, rq, skv, rkv, ms, mr, ps, pr, lc0, lc1, rl, tt, mx, mxs, mxr, qpad,
-    loc_sem, x_sem, w_sem, q_sem, kv_sem, ring_send, ring_recv, m_sem, a_sem,
+    wqkv_ref, table_ref, lens_ref, freq_ref, deal_ref, mig_ref, kv, vt, g, xall, wall, sq, rq, skv, skv_out, rkv, ms, mr, ps, pr, lc0, lc1, rl, tt, mx, mxs, mxr, qpad,
+    loc_sem, x_sem, w_sem, q_sem, kv_send, kv_recv, ring_send, ring_recv, m_sem, a_sem,
 ):
     me_r = lax.axis_index("row")
     me_c = lax.axis_index("col")
@@ -144,6 +144,33 @@
             lax.fori_loop(0, half_slots, fill, 0)
             ring_copy(sign, half, hop).start()
 
+    def kv_copy(sign, half, hop):
+        return pltpu.make_async_remote_copy(
+            src_ref=skv_out.at[sign, half, hop], dst_ref=rkv.at[sign, half, hop],
+            send_sem=kv_send.at[sign, half, hop], recv_sem=kv_recv.at[sign, half, hop],
+            device_id={"row": left if sign == 0 else right}, device_id_type=MESH,
+        )
+
+    def kv_hop(hop):
+        for sign in (0, 1):
+            for half in (sign, 1 - sign):
+                if hop < hops(sign, half):
+                    dist = hops(sign, half) - hop
+                    block = lax.rem(me_r + (rows - dist if sign == 0 else dist), rows)
+                    part = skv[block, half * HD : (half + 1) * HD]
+                    if hop > 0:
+                        kv_copy(sign, half, hop - 1).wait_recv()
+                        part = (part.astype(F32) + rkv[sign, half, hop - 1].astype(F32)).astype(BF)
+                    skv_out[sign, half, hop] = part
+                    kv_copy(sign, half, hop).start()
+
+    def kv_sum(half):
+        summed = skv[me_r, half * HD : (half + 1) * HD].astype(F32)
+        for sign in (0, 1):
+            kv_copy(sign, half, hops(sign, half) - 1).wait_recv()
+            summed = summed + rkv[sign, half, hops(sign, half) - 1].astype(F32)
+        return summed
+
     for copy in small:
         copy.wait()
     for copy in pool_copies:
@@ -153,13 +180,15 @@
 
     lens = lens_ref[...]
 
+    half_rows = slot_rows // 2
     lanes = iota((128, 128), 1).astype(F32)
     for jb in range(total // 128):
         column = jnp.broadcast_to(deal_ref[jb : jb + 1, :].astype(F32), (128, 128)).T
         for ib in range(total // 128):
-            g[jb * 128 : jb * 128 + 128, ib * 128 : ib * 128 + 128] = jnp.where(
-                column == lanes + float(ib * 128), 1.0, 0.0
-            ).astype(BF)
+            hit = jnp.where(column == lanes + float(ib * 128), 1.0, 0.0).astype(BF)
+            for n in range(128 // half_rows):
+                at = (jb * 128 // half_rows + n) // 2 * half_rows
+                g[n % 2, at : at + half_rows, ib * 128 : ib * 128 + 128] = hit[n * half_rows : (n + 1) * half_rows]
 
     angles = freq_ref[...] * lens.astype(F32)
     cosine = jnp.cos(angles)
@@ -195,19 +224,26 @@
         vt[c] = dot(pick, tokens, NT).astype(BF)
         return carry
 
-    lax.fori_loop(0, pages // CHUNK, turn, 0)
-
     wait_all(xall, cols - 1, x_sem.at[1])
-    projected = dot(wqkv_ref[...], xall[...].reshape(total, xn_ref.shape[1]), NT).astype(BF)
+    projected = [
+        dot(
+            wqkv_ref[...],
+            xall[:, part * half_rows : (part + 1) * half_rows].reshape(total // 2, xn_ref.shape[1]),
+            NT,
+        ).astype(BF)
+        for part in (0, 1)
+    ]
     for b in range(rows):
-        block = dot(projected, g[:, b * reqs : (b + 1) * reqs]).astype(BF)
+        cut = slice(b * reqs, (b + 1) * reqs)
+        block = (dot(projected[0], g[0, :, cut]) + dot(projected[1], g[1, :, cut])).astype(BF)
         sq[b] = block[:HD]
         skv[b] = block[HD:]
     to_rows(lambda to: sq.at[to], rq.at[me_r], q_sem)
-    to_rows(lambda to: skv.at[to], rkv.at[me_r], kv_sem)
+    kv_hop(0)
 
     ring_hop(1, False)
     to_cols(lambda to: wout_ref, wall.at[me_c], w_sem)
+    lax.fori_loop(0, pages // CHUNK, turn, 0)
 
     def rotate(x):
         u, w = x[: HD // 2], x[HD // 2 :]
@@ -241,20 +277,18 @@
 
     carry = (jnp.full((1, reqs), START, F32), jnp.zeros((1, reqs), F32), jnp.zeros((HD, reqs), F32))
     chunks = pages // CHUNK
+    kv_hop(1)
     ring_hop(2, True)
     carry = lax.fori_loop(0, chunks // 2, chunk, carry)
+    kv_hop(2)
     ring_hop(2, False)
     carry = lax.fori_loop(chunks // 2, chunks, chunk, carry)
 
-    wait_all(rkv, rows - 1, kv_sem.at[1])
-    summed = skv[me_r].astype(F32)
-    for o in range(1, rows):
-        summed = summed + rkv[lax.rem(me_r + o, rows)].astype(F32)
-    key_new = rotate(summed[:HD])
-    value_new = summed[HD:].astype(BF)
-
+    kv_hop(3)
     ring_hop(3, True)
 
+    key_new = rotate(kv_sum(0))
+    value_new = kv_sum(1).astype(BF)
     top, norm, acc = carry
     score_new = jnp.sum(query.astype(F32) * key_new.astype(F32), axis=0, keepdims=True) * 0.125
     new_top = jnp.maximum(top, score_new)
@@ -289,29 +323,39 @@
     to_rows(lambda to: mx.at[me_r], mx.at[me_r], m_sem)
     wait_all(mx, rows - 1, m_sem.at[1])
     heads = jnp.concatenate([mx[b] for b in range(rows)], axis=1)
-    odd = lax.rem(me_c, 2)
     none = jnp.zeros_like(heads)
-    placed = jnp.concatenate(
-        [jnp.where(odd == 0, heads, none), jnp.where(odd == 0, none, heads)], axis=0
+    packed = dot(g[0], jnp.concatenate([heads, none], axis=0), NT) + dot(
+        g[1], jnp.concatenate([none, heads], axis=0), NT
     )
-    mxs[...] = dot(g[...], placed, NT).astype(BF).reshape(mxs.shape)
+    mxs[...] = packed.astype(BF).reshape(mxs.shape)
     to_cols(lambda to: mxs.at[to], mxr.at[me_c], a_sem)
     mxr[me_c] = mxs[me_c]
     wait_all(wall, cols - 1, w_sem.at[1])
     wait_all(mxr, cols - 1, a_sem.at[1])
-    pairs = jnp.concatenate([mxr[2 * k] + mxr[2 * k + 1] for k in range(cols // 2)], axis=1)
+    even = jnp.concatenate([mxr[2 * k] for k in range(cols // 2)], axis=0).astype(F32)
+    odd = jnp.concatenate([mxr[2 * k + 1] for k in range(cols // 2)], axis=0).astype(F32)
+    first = iota(even.shape, 1) < HD
+    low = jnp.where(first, even, pltpu.roll(odd, HD, 1)).astype(BF)
+    high = jnp.where(first, pltpu.roll(even, HD, 1), odd).astype(BF)
+    pairs = jnp.concatenate(
+        [
+            jnp.concatenate([x[k * half_rows : (k + 1) * half_rows] for k in range(cols // 2)], axis=1)
+            for x in (low, high)
+        ],
+        axis=0,
+    )
     att_ref[...] = dot(pairs, wall[...].reshape(cols * HD, wout_ref.shape[1])).astype(BF)
 
     wait_all(xall, cols - 1, x_sem.at[0])
     wait_all(wall, cols - 1, w_sem.at[0])
     wait_all(rq, rows - 1, q_sem.at[0])
-    wait_all(rkv, rows - 1, kv_sem.at[0])
     wait_all(mx, rows - 1, m_sem.at[0])
     wait_all(mxr, cols - 1, a_sem.at[0])
     for sign in (0, 1):
         for half in (0, 1):
             for hop in range(hops(sign, half)):
                 ring_copy(sign, half, hop).wait_send()
+                kv_copy(sign, half, hop).wait_send()
     landed_copy.wait()
 
 
@@ -344,13 +388,14 @@
             pltpu.SMEM(mig_src.shape, jnp.int32),
             pltpu.VMEM((pages + slots, page, lanes), BF),
             pltpu.VMEM(((pages + slots) // CHUNK, HD, CHUNK * page), BF),
-            pltpu.VMEM((total, total), BF),
+            pltpu.VMEM((2, total // 2, total), BF),
             pltpu.VMEM((cols, slot_rows, depth), BF),
             pltpu.VMEM((cols, HD, w_out.shape[1]), BF),
             pltpu.VMEM((rows, HD, reqs), BF),
             pltpu.VMEM((rows, HD, reqs), BF),
             pltpu.VMEM((rows, 2 * HD, reqs), BF),
-            pltpu.VMEM((rows, 2 * HD, reqs), BF),
+            pltpu.VMEM((2, 2, far, HD, reqs), BF),
+            pltpu.VMEM((2, 2, far, HD, reqs), BF),
             pltpu.VMEM((2, far, slots // 2, page, lanes), BF),
             pltpu.VMEM((2, far, slots // 2, page, lanes), BF),
             pltpu.VMEM((2, far, slots // 2, page, lanes), BF),
@@ -360,10 +405,10 @@
             pltpu.VMEM((pages + slots, reqs), F32),
             pltpu.VMEM((page_table.shape[1], reqs), F32),
             pltpu.VMEM((rows, HD, reqs), BF),
-            pltpu.VMEM((cols, slot_rows, 2 * HD), BF),
-            pltpu.VMEM((cols, slot_rows, 2 * HD), BF),
+            pltpu.VMEM((cols, slot_rows // 2, 2 * HD), BF),
+            pltpu.VMEM((cols, slot_rows // 2, 2 * HD), BF),
             pltpu.VMEM((2 * HD, reqs), BF),
-            dma((14,)), dma((2,)), dma((2,)), dma((2,)), dma((2,)),
+            dma((14,)), dma((2,)), dma((2,)), dma((2,)), dma((2, 2, far)), dma((2, 2, far)),
             dma((2, 2, far)), dma((2, 2, far)), dma((2,)), dma((2,)),
         ],
         compiler_params=pltpu.CompilerParams(

time: 64.4 us -> 61 us (0.947)
  Pallas kernels: 60.6 us -> 57.2 us
    pallas_call x1, Pallas kernels: 60.6 us -> 57.2 us  [on_device(): pl.pallas_call(functools.partial(kernel, rows, cols), out_shape=(jax.Shap...]
where the time goes in v3:
time: 61 us; the launch traced here: 60.9 us
  Pallas kernels  57.2 us (94%)
  local copies, waits for them, and re-layouts  2.99 us (5%)
  between operations  0.64 us (1%)
    pallas_call x1, Pallas kernels, on_device(): pl.pallas_call(functools.partial(kernel, rows, cols), out_shape=(jax.Shap...  57.2 us
    unnamed x2, local copies, waits for them, and re-layouts  2.99 us

profile of v3, /device:TPU:1, one launch (start us, length us, event | category | flops | bytes accessed | tf_op | source)
XLA Modules:
  0.0 60.9 jit_solution(1382521721730310605)
XLA Ops:
  0.6 57.2 %shard_map.104 = (bf16[32,256]{1,0:T(8,128)(2,1)}, bf16[16,64,128]{2,1,0:T(8,128)(2,1)}) custom-call(bf16[32,256]{1,0:T(8,128)(2,1)} %xn_ref.1, bf16[192,256]{1,0:T(8,128)(2,1)} %bitcast.4, bf16[64,256]{1,0:T(8,128)(2,1)} %wout_ref.1, bf16[256,64,128]{2,1,0:T(8,128)(2,1)} %pool_ref.1, s32[64,128]{1,0:T(8,128)} %bitcast.5, s32[1,128]{1,0:T(1,128)} %bitcast.7, ...), custom_call_target="tpu_custom_call" | custom-call | tf_op jit(solution)/shard_map/pallas_call | solution.py:374
  57.9 1.3 %copy.13 = bf16[32,256]{1,0:T(8,128)(2,1)} copy(bf16[32,256]{1,0:T(8,128)(2,1)} %get-tuple-element.4) | data formatting | bytes 32768
  59.2 1.7 %copy.14 = bf16[16,64,128]{2,1,0:T(8,128)(2,1)} copy(bf16[16,64,128]{2,1,0:T(8,128)(2,1)} %get-tuple-element.5) | data formatting | bytes 524288

commit v4 on v3

--- a/solution.py
+++ b/solution.py
@@ -34,7 +34,7 @@
     rows, cols,
     xn_ref, wqkv_hbm, wout_ref, pool_ref, table_hbm, lens_hbm, freq_hbm, deal_hbm, mig_hbm,
     att_ref, landed_ref,
-    wqkv_ref, table_ref, lens_ref, freq_ref, deal_ref, mig_ref, kv, vt, g, xall, wall, sq, rq, skv, skv_out, rkv, ms, mr, ps, pr, lc0, lc1, rl, tt, mx, mxs, mxr, qpad,
+    wqkv_ref, table_ref, lens_ref, freq_ref, deal_ref, mig_ref, kv, vt, g, xall, wall, sq, rq, skv, kv_out, rkv, ms, mr, ps, pr, lc0, lc1, rl, tt, mx, mxs, mxr, qpad,
     loc_sem, x_sem, w_sem, q_sem, kv_send, kv_recv, ring_send, ring_recv, m_sem, a_sem,
 ):
     me_r = lax.axis_index("row")
@@ -61,7 +61,7 @@
         pltpu.make_async_copy(src, dst, loc_sem.at[2 + n])
         for n, (src, dst) in enumerate((
             (mig_hbm, mig_ref), (lens_hbm, lens_ref), (table_hbm, table_ref), (deal_hbm, deal_ref),
-            (freq_hbm, freq_ref), (wqkv_hbm, wqkv_ref), (xn_ref, xall.at[me_c]), (wout_ref, wall.at[me_c]),
+            (freq_hbm, freq_ref), (wqkv_hbm, wqkv_ref), (xn_ref, xall.at[lax.rem(me_c, 2), me_c // 2]), (wout_ref, wall.at[me_c]),
         ))
     ]
     for copy in small:
@@ -107,7 +107,22 @@
         part = buf.at[pl.ds(0, count)]
         pltpu.make_async_copy(part, part, sem).wait()
 
-    to_cols(lambda to: xn_ref, xall.at[me_c], x_sem)
+    core = lax.rem(me_c, 2)
+    chip = me_c // 2
+    sibling = me_c + 1 - 2 * core
+
+    def to_chip(o, carry):
+        pltpu.make_async_remote_copy(
+            src_ref=xn_ref, dst_ref=xall.at[core, chip], send_sem=x_sem.at[0], recv_sem=x_sem.at[1],
+            device_id={"col": lax.rem(me_c + 2 * o, cols)}, device_id_type=MESH,
+        ).start()
+        return carry
+
+    lax.fori_loop(1, cols // 2, to_chip, 0)
+    x_share = pltpu.make_async_remote_copy(
+        src_ref=xall.at[core], dst_ref=xall.at[core], send_sem=x_sem.at[2], recv_sem=x_sem.at[3],
+        device_id={"col": sibling}, device_id_type=MESH,
+    )
 
     left = lax.rem(me_r + rows - 1, rows)
     right = lax.rem(me_r + 1, rows)
@@ -144,31 +159,43 @@
             lax.fori_loop(0, half_slots, fill, 0)
             ring_copy(sign, half, hop).start()
 
-    def kv_copy(sign, half, hop):
+    def row_at(shift):
+        return lax.rem(me_r + rows + shift, rows)
+
+    def half_of(block, half):
+        return skv.at[row_at(block), pl.ds(half * HD, HD)]
+
+    def kv_copy(half, slot):
+        s = 1 - 2 * half
+        block, to = ((-4, -2), (-3, -1), (3, 1), (-1, -1), (1, 1), (None, -2), (None, 2))[slot]
         return pltpu.make_async_remote_copy(
-            src_ref=skv_out.at[sign, half, hop], dst_ref=rkv.at[sign, half, hop],
-            send_sem=kv_send.at[sign, half, hop], recv_sem=kv_recv.at[sign, half, hop],
-            device_id={"row": left if sign == 0 else right}, device_id_type=MESH,
+            src_ref=kv_out.at[half, slot - 5] if block is None else half_of(block * s, half),
+            dst_ref=rkv.at[half, slot],
+            send_sem=kv_send.at[half, slot], recv_sem=kv_recv.at[half, slot],
+            device_id={"row": row_at(to * s)}, device_id_type=MESH,
         )
 
-    def kv_hop(hop):
-        for sign in (0, 1):
-            for half in (sign, 1 - sign):
-                if hop < hops(sign, half):
-                    dist = hops(sign, half) - hop
-                    block = lax.rem(me_r + (rows - dist if sign == 0 else dist), rows)
-                    part = skv[block, half * HD : (half + 1) * HD]
-                    if hop > 0:
-                        kv_copy(sign, half, hop - 1).wait_recv()
-                        part = (part.astype(F32) + rkv[sign, half, hop - 1].astype(F32)).astype(BF)
-                    skv_out[sign, half, hop] = part
-                    kv_copy(sign, half, hop).start()
+    def kv_first():
+        for slot in range(5):
+            for half in (0, 1):
+                kv_copy(half, slot).start()
+
+    def kv_second():
+        for half in (0, 1):
+            s = 1 - 2 * half
+            for slot, side, parts in ((5, -2 * s, (0, 1)), (6, 2 * s, (2,))):
+                summed = half_of(side, half)[...].astype(F32)
+                for part in parts:
+                    kv_copy(half, part).wait_recv()
+                    summed = summed + rkv[half, part].astype(F32)
+                kv_out[half, slot - 5] = summed.astype(BF)
+                kv_copy(half, slot).start()
 
     def kv_sum(half):
-        summed = skv[me_r, half * HD : (half + 1) * HD].astype(F32)
-        for sign in (0, 1):
-            kv_copy(sign, half, hops(sign, half) - 1).wait_recv()
-            summed = summed + rkv[sign, half, hops(sign, half) - 1].astype(F32)
+        summed = half_of(0, half)[...].astype(F32)
+        for slot in range(3, 7):
+            kv_copy(half, slot).wait_recv()
+            summed = summed + rkv[half, slot].astype(F32)
         return summed
 
     for copy in small:
@@ -187,7 +214,8 @@
         for ib in range(total // 128):
             hit = jnp.where(column == lanes + float(ib * 128), 1.0, 0.0).astype(BF)
             for n in range(128 // half_rows):
-                at = (jb * 128 // half_rows + n) // 2 * half_rows
+                c = (jb * 128 // half_rows + n) // 2
+                at = (c % 2 * (cols // 2) + c // 2) * half_rows
                 g[n % 2, at : at + half_rows, ib * 128 : ib * 128 + 128] = hit[n * half_rows : (n + 1) * half_rows]
 
     angles = freq_ref[...] * lens.astype(F32)
@@ -215,8 +243,6 @@
         lc1[where, :] = jnp.log(count + 1.0)
         rl[where, :] = jnp.where(last == ids, rest, 0.0)
 
-    ring_hop(1, True)
-
     pick = jnp.where(iota((HD, 2 * HD), 0) + HD == iota((HD, 2 * HD), 1), 1.0, 0.0).astype(BF)
 
     def turn(c, carry):
@@ -224,11 +250,18 @@
         vt[c] = dot(pick, tokens, NT).astype(BF)
         return carry
 
-    wait_all(xall, cols - 1, x_sem.at[1])
+    lax.fori_loop(0, pages // CHUNK // 2, turn, 0)
+    ring_hop(1, True)
+    lax.fori_loop(pages // CHUNK // 2, pages // CHUNK, turn, 0)
+
+    ring_hop(1, False)
+    wait_all(xall.at[0], cols // 2 - 1, x_sem.at[1])
+    x_share.start()
+    x_share.wait_recv()
     projected = [
         dot(
             wqkv_ref[...],
-            xall[:, part * half_rows : (part + 1) * half_rows].reshape(total // 2, xn_ref.shape[1]),
+            xall[:, :, part * half_rows : (part + 1) * half_rows].reshape(total // 2, xn_ref.shape[1]),
             NT,
         ).astype(BF)
         for part in (0, 1)
@@ -239,11 +272,10 @@
         sq[b] = block[:HD]
         skv[b] = block[HD:]
     to_rows(lambda to: sq.at[to], rq.at[me_r], q_sem)
-    kv_hop(0)
-
-    ring_hop(1, False)
+    kv_first()
+    ring_hop(2, True)
     to_cols(lambda to: wout_ref, wall.at[me_c], w_sem)
-    lax.fori_loop(0, pages // CHUNK, turn, 0)
+    ring_hop(2, False)
 
     def rotate(x):
         u, w = x[: HD // 2], x[HD // 2 :]
@@ -256,6 +288,7 @@
     query = rotate(summed)
     qpad[...] = jnp.concatenate([query * jnp.asarray(0.125, BF), jnp.zeros((HD, reqs), BF)], axis=0)
 
+    kv_second()
     offsets = iota((PAGE, reqs), 0).astype(F32)
 
     def chunk(c, carry):
@@ -277,15 +310,9 @@
 
     carry = (jnp.full((1, reqs), START, F32), jnp.zeros((1, reqs), F32), jnp.zeros((HD, reqs), F32))
     chunks = pages // CHUNK
-    kv_hop(1)
-    ring_hop(2, True)
     carry = lax.fori_loop(0, chunks // 2, chunk, carry)
-    kv_hop(2)
-    ring_hop(2, False)
+    ring_hop(3, True)
     carry = lax.fori_loop(chunks // 2, chunks, chunk, carry)
-
-    kv_hop(3)
-    ring_hop(3, True)
 
     key_new = rotate(kv_sum(0))
     value_new = kv_sum(1).astype(BF)
@@ -328,8 +355,8 @@
         g[1], jnp.concatenate([none, heads], axis=0), NT
     )
     mxs[...] = packed.astype(BF).reshape(mxs.shape)
-    to_cols(lambda to: mxs.at[to], mxr.at[me_c], a_sem)
-    mxr[me_c] = mxs[me_c]
+    to_cols(lambda to: mxs.at[lax.rem(to, 2) * (cols // 2) + to // 2], mxr.at[me_c], a_sem)
+    mxr[me_c] = mxs[core * (cols // 2) + chip]
     wait_all(wall, cols - 1, w_sem.at[1])
     wait_all(mxr, cols - 1, a_sem.at[1])
     even = jnp.concatenate([mxr[2 * k] for k in range(cols // 2)], axis=0).astype(F32)
@@ -346,7 +373,8 @@
     )
     att_ref[...] = dot(pairs, wall[...].reshape(cols * HD, wout_ref.shape[1])).astype(BF)
 
-    wait_all(xall, cols - 1, x_sem.at[0])
+    wait_all(xall.at[0], cols // 2 - 1, x_sem.at[0])
+    x_share.wait_send()
     wait_all(wall, cols - 1, w_sem.at[0])
     wait_all(rq, rows - 1, q_sem.at[0])
     wait_all(mx, rows - 1, m_sem.at[0])
@@ -355,11 +383,13 @@
         for half in (0, 1):
             for hop in range(hops(sign, half)):
                 ring_copy(sign, half, hop).wait_send()
-                kv_copy(sign, half, hop).wait_send()
+    for half in (0, 1):
+        for slot in range(7):
+            kv_copy(half, slot).wait_send()
     landed_copy.wait()
 
 
-def on_device(rows, cols, interpret, xn, w_qkv, w_out, pool, page_table, lengths, mig_src, deal):
+def on_device(rows, cols, xn, w_qkv, w_out, pool, page_table, lengths, mig_src, deal):
     reqs = lengths.shape[0]
     pages, page, lanes = pool.shape
     slots = mig_src.shape[0] // rows
@@ -389,13 +419,13 @@
             pltpu.VMEM((pages + slots, page, lanes), BF),
             pltpu.VMEM(((pages + slots) // CHUNK, HD, CHUNK * page), BF),
             pltpu.VMEM((2, total // 2, total), BF),
-            pltpu.VMEM((cols, slot_rows, depth), BF),
+            pltpu.VMEM((2, cols // 2, slot_rows, depth), BF),
             pltpu.VMEM((cols, HD, w_out.shape[1]), BF),
             pltpu.VMEM((rows, HD, reqs), BF),
             pltpu.VMEM((rows, HD, reqs), BF),
             pltpu.VMEM((rows, 2 * HD, reqs), BF),
-            pltpu.VMEM((2, 2, far, HD, reqs), BF),
-            pltpu.VMEM((2, 2, far, HD, reqs), BF),
+            pltpu.VMEM((2, 2, HD, reqs), BF),
+            pltpu.VMEM((2, 7, HD, reqs), BF),
             pltpu.VMEM((2, far, slots // 2, page, lanes), BF),
             pltpu.VMEM((2, far, slots // 2, page, lanes), BF),
             pltpu.VMEM((2, far, slots // 2, page, lanes), BF),
@@ -408,7 +438,7 @@
             pltpu.VMEM((cols, slot_rows // 2, 2 * HD), BF),
             pltpu.VMEM((cols, slot_rows // 2, 2 * HD), BF),
             pltpu.VMEM((2 * HD, reqs), BF),
-            dma((14,)), dma((2,)), dma((2,)), dma((2,)), dma((2, 2, far)), dma((2, 2, far)),
+            dma((14,)), dma((4,)), dma((2,)), dma((2,)), dma((2, 7)), dma((2, 7)),
             dma((2, 2, far)), dma((2, 2, far)), dma((2,)), dma((2,)),
         ],
         compiler_params=pltpu.CompilerParams(
@@ -419,7 +449,7 @@
 
 def solution(mesh):
     return jax.shard_map(
-        functools.partial(on_device, mesh.shape["row"], mesh.shape["col"], False),
+        functools.partial(on_device, mesh.shape["row"], mesh.shape["col"]),
         mesh=mesh,
         in_specs=(
             P("col", "row"),

time: 61 us -> 58 us (0.951)
  Pallas kernels: 57.2 us -> 54.2 us
    pallas_call x1, Pallas kernels: 57.2 us -> 54.2 us  [on_device(): pl.pallas_call(functools.partial(kernel, rows, cols), out_shape=(jax.Shap...]
where the time goes in v4:
time: 58 us; the launch traced here: 57.8 us
  Pallas kernels  54.2 us (93%)
  local copies, waits for them, and re-layouts  2.99 us (5%)
  between operations  0.64 us (1%)
    pallas_call x1, Pallas kernels, on_device(): pl.pallas_call(functools.partial(kernel, rows, cols), out_shape=(jax.Shap...  54.2 us
    unnamed x2, local copies, waits for them, and re-layouts  2.99 us

profile of v4, /device:TPU:1, one launch (start us, length us, event | category | flops | bytes accessed | tf_op | source)
XLA Modules:
  0.0 57.8 jit_solution(9350168887858575890)
XLA Ops:
  0.6 54.2 %shard_map.104 = (bf16[32,256]{1,0:T(8,128)(2,1)}, bf16[16,64,128]{2,1,0:T(8,128)(2,1)}) custom-call(bf16[32,256]{1,0:T(8,128)(2,1)} %xn_ref.1, bf16[192,256]{1,0:T(8,128)(2,1)} %bitcast.4, bf16[64,256]{1,0:T(8,128)(2,1)} %wout_ref.1, bf16[256,64,128]{2,1,0:T(8,128)(2,1)} %pool_ref.1, s32[64,128]{1,0:T(8,128)} %bitcast.5, s32[1,128]{1,0:T(1,128)} %bitcast.7, ...), custom_call_target="tpu_custom_call" | custom-call | tf_op jit(solution)/shard_map/pallas_call | solution.py:404
  54.8 1.3 %copy.13 = bf16[32,256]{1,0:T(8,128)(2,1)} copy(bf16[32,256]{1,0:T(8,128)(2,1)} %get-tuple-element.4) | data formatting | bytes 32768
  56.2 1.7 %copy.14 = bf16[16,64,128]{2,1,0:T(8,128)(2,1)} copy(bf16[16,64,128]{2,1,0:T(8,128)(2,1)} %get-tuple-element.5) | data formatting | bytes 524288

commit v5 on v4

--- a/solution.py
+++ b/solution.py
@@ -61,7 +61,7 @@
         pltpu.make_async_copy(src, dst, loc_sem.at[2 + n])
         for n, (src, dst) in enumerate((
             (mig_hbm, mig_ref), (lens_hbm, lens_ref), (table_hbm, table_ref), (deal_hbm, deal_ref),
-            (freq_hbm, freq_ref), (wqkv_hbm, wqkv_ref), (xn_ref, xall.at[lax.rem(me_c, 2), me_c // 2]), (wout_ref, wall.at[me_c]),
+            (freq_hbm, freq_ref), (wqkv_hbm, wqkv_ref), (xn_ref, xall.at[lax.rem(me_c, 2), me_c // 2]), (wout_ref, wall.at[lax.rem(me_c, 2), me_c // 2]),
         ))
     ]
     for copy in small:
@@ -79,8 +79,8 @@
         pl.semaphore_signal(barrier, inc=1, device_id={"row": lax.rem(me_r + o, rows)}, device_id_type=MESH)
         return carry
 
-    lax.fori_loop(1, cols, greet_col, 0)
-    lax.fori_loop(1, rows, greet_row, 0)
+    lax.fori_loop(1, cols, greet_col, 0, unroll=True)
+    lax.fori_loop(1, rows, greet_row, 0, unroll=True)
     pl.semaphore_wait(barrier, cols + rows - 2)
 
     def to_cols(src, dst, sems):
@@ -91,7 +91,7 @@
                 device_id={"col": to}, device_id_type=MESH,
             ).start()
             return carry
-        lax.fori_loop(1, cols, send, 0)
+        lax.fori_loop(1, cols, send, 0, unroll=True)
 
     def to_rows(src, dst, sems):
         def send(o, carry):
@@ -101,7 +101,7 @@
                 device_id={"row": to}, device_id_type=MESH,
             ).start()
             return carry
-        lax.fori_loop(1, rows, send, 0)
+        lax.fori_loop(1, rows, send, 0, unroll=True)
 
     def wait_all(buf, count, sem):
         part = buf.at[pl.ds(0, count)]
@@ -111,18 +111,24 @@
     chip = me_c // 2
     sibling = me_c + 1 - 2 * core
 
-    def to_chip(o, carry):
-        pltpu.make_async_remote_copy(
-            src_ref=xn_ref, dst_ref=xall.at[core, chip], send_sem=x_sem.at[0], recv_sem=x_sem.at[1],
-            device_id={"col": lax.rem(me_c + 2 * o, cols)}, device_id_type=MESH,
-        ).start()
-        return carry
-
-    lax.fori_loop(1, cols // 2, to_chip, 0)
-    x_share = pltpu.make_async_remote_copy(
-        src_ref=xall.at[core], dst_ref=xall.at[core], send_sem=x_sem.at[2], recv_sem=x_sem.at[3],
-        device_id={"col": sibling}, device_id_type=MESH,
-    )
+    def to_chips(src, buf, sems):
+        def send(o, carry):
+            pltpu.make_async_remote_copy(
+                src_ref=src, dst_ref=buf.at[core, chip], send_sem=sems.at[0], recv_sem=sems.at[1],
+                device_id={"col": lax.rem(me_c + 2 * o, cols)}, device_id_type=MESH,
+            ).start()
+            return carry
+        lax.fori_loop(1, cols // 2, send, 0, unroll=True)
+
+    def share(buf, sems):
+        return pltpu.make_async_remote_copy(
+            src_ref=buf.at[core], dst_ref=buf.at[core], send_sem=sems.at[2], recv_sem=sems.at[3],
+            device_id={"col": sibling}, device_id_type=MESH,
+        )
+
+    to_chips(xn_ref, xall, x_sem)
+    x_share = share(xall, x_sem)
+    w_share = share(wall, w_sem)
 
     left = lax.rem(me_r + rows - 1, rows)
     right = lax.rem(me_r + 1, rows)
@@ -156,7 +162,7 @@
                 out[half, hop, t] = page
                 return carry
 
-            lax.fori_loop(0, half_slots, fill, 0)
+            lax.fori_loop(0, half_slots, fill, 0, unroll=True)
             ring_copy(sign, half, hop).start()
 
     def row_at(shift):
@@ -274,7 +280,7 @@
     to_rows(lambda to: sq.at[to], rq.at[me_r], q_sem)
     kv_first()
     ring_hop(2, True)
-    to_cols(lambda to: wout_ref, wall.at[me_c], w_sem)
+    to_chips(wout_ref, wall, w_sem)
     ring_hop(2, False)
 
     def rotate(x):
@@ -324,6 +330,8 @@
     norm = norm * scale + weight_new
     acc = acc * scale + weight_new.astype(BF).astype(F32) * value_new.astype(F32)
 
+    wait_all(wall.at[0], cols // 2 - 1, w_sem.at[1])
+    w_share.start()
     for half in (1, 0):
         for sign in (0, 1):
             side = half if sign == 0 else 1 - half
@@ -357,10 +365,11 @@
     mxs[...] = packed.astype(BF).reshape(mxs.shape)
     to_cols(lambda to: mxs.at[lax.rem(to, 2) * (cols // 2) + to // 2], mxr.at[me_c], a_sem)
     mxr[me_c] = mxs[core * (cols // 2) + chip]
-    wait_all(wall, cols - 1, w_sem.at[1])
+    w_share.wait_recv()
     wait_all(mxr, cols - 1, a_sem.at[1])
-    even = jnp.concatenate([mxr[2 * k] for k in range(cols // 2)], axis=0).astype(F32)
-    odd = jnp.concatenate([mxr[2 * k + 1] for k in range(cols // 2)], axis=0).astype(F32)
+    order = [2 * n + side for side in (0, 1) for n in range(cols // 2)]
+    even = jnp.concatenate([mxr[c] for c in order[0::2]], axis=0).astype(F32)
+    odd = jnp.concatenate([mxr[c] for c in order[1::2]], axis=0).astype(F32)
     first = iota(even.shape, 1) < HD
     low = jnp.where(first, even, pltpu.roll(odd, HD, 1)).astype(BF)
     high = jnp.where(first, pltpu.roll(even, HD, 1), odd).astype(BF)
@@ -375,7 +384,8 @@
 
     wait_all(xall.at[0], cols // 2 - 1, x_sem.at[0])
     x_share.wait_send()
-    wait_all(wall, cols - 1, w_sem.at[0])
+    wait_all(wall.at[0], cols // 2 - 1, w_sem.at[0])
+    w_share.wait_send()
     wait_all(rq, rows - 1, q_sem.at[0])
     wait_all(mx, rows - 1, m_sem.at[0])
     wait_all(mxr, cols - 1, a_sem.at[0])
@@ -420,7 +430,7 @@
             pltpu.VMEM(((pages + slots) // CHUNK, HD, CHUNK * page), BF),
             pltpu.VMEM((2, total // 2, total), BF),
             pltpu.VMEM((2, cols // 2, slot_rows, depth), BF),
-            pltpu.VMEM((cols, HD, w_out.shape[1]), BF),
+            pltpu.VMEM((2, cols // 2, HD, w_out.shape[1]), BF),
             pltpu.VMEM((rows, HD, reqs), BF),
             pltpu.VMEM((rows, HD, reqs), BF),
             pltpu.VMEM((rows, 2 * HD, reqs), BF),
@@ -438,7 +448,7 @@
             pltpu.VMEM((cols, slot_rows // 2, 2 * HD), BF),
             pltpu.VMEM((cols, slot_rows // 2, 2 * HD), BF),
             pltpu.VMEM((2 * HD, reqs), BF),
-            dma((14,)), dma((4,)), dma((2,)), dma((2,)), dma((2, 7)), dma((2, 7)),
+            dma((14,)), dma((4,)), dma((4,)), dma((2,)), dma((2, 7)), dma((2, 7)),
             dma((2, 2, far)), dma((2, 2, far)), dma((2,)), dma((2,)),
         ],
         compiler_params=pltpu.CompilerParams(

time: 58 us -> 57.5 us (level)
  no operation moved by 1% of the time
where the time goes in v5:
time: 57.5 us; the launch traced here: 57.3 us
  Pallas kernels  53.7 us (93%)
  local copies, waits for them, and re-layouts  2.99 us (5%)
  between operations  0.64 us (1%)
    pallas_call x1, Pallas kernels, on_device(): pl.pallas_call(functools.partial(kernel, rows, cols), out_shape=(jax.Shap...  53.7 us
    unnamed x2, local copies, waits for them, and re-layouts  2.99 us

profile of v5, /device:TPU:1, one launch (start us, length us, event | category | flops | bytes accessed | tf_op | source)
XLA Modules:
  0.0 57.3 jit_solution(4506748179713874988)
XLA Ops:
  0.6 53.7 %shard_map.104 = (bf16[32,256]{1,0:T(8,128)(2,1)}, bf16[16,64,128]{2,1,0:T(8,128)(2,1)}) custom-call(bf16[32,256]{1,0:T(8,128)(2,1)} %xn_ref.1, bf16[192,256]{1,0:T(8,128)(2,1)} %bitcast.4, bf16[64,256]{1,0:T(8,128)(2,1)} %wout_ref.1, bf16[256,64,128]{2,1,0:T(8,128)(2,1)} %pool_ref.1, s32[64,128]{1,0:T(8,128)} %bitcast.5, s32[1,128]{1,0:T(1,128)} %bitcast.7, ...), custom_call_target="tpu_custom_call" | custom-call | tf_op jit(solution)/shard_map/pallas_call | solution.py:414
  54.3 1.3 %copy.13 = bf16[32,256]{1,0:T(8,128)(2,1)} copy(bf16[32,256]{1,0:T(8,128)(2,1)} %get-tuple-element.4) | data formatting | bytes 32768
  55.7 1.7 %copy.14 = bf16[16,64,128]{2,1,0:T(8,128)(2,1)} copy(bf16[16,64,128]{2,1,0:T(8,128)(2,1)} %get-tuple-element.5) | data formatting | bytes 524288
